TPU v7x, 32 devices: a whole 2x2x4 slice. The times are simulated.
32 devices in a mesh: groups: 2 (over x), seg: 16 (over z, y, core).
Axes of the slice: x: 2, y: 2, z: 4, core: 2. Of those that a mesh axis runs over, the one named last changes fastest.
Arguments:
- points: bfloat16 [16, 262144], P(None, ('groups', 'seg')), parts along dimension 1, may hold values from -6 to 6
- vectors: bfloat16 [32, 262144], P(None, ('groups', 'seg')), parts along dimension 1, may hold values from -6 to 6
- lengthscale: float32 [32], P('groups'), parts along dimension 0, may hold values from 1.5 to 4
- leaf_basis: bfloat16 [512, 64, 512], P(('groups', 'seg')), parts along dimension 0, may hold values from -0.25 to 0.25
- local_transfer: bfloat16 [960, 64, 64], P(('groups', 'seg')), parts along dimension 0, may hold values from -0.625 to 0.625
- upper_transfer: bfloat16 [48, 64, 64], P('groups'), parts along dimension 0, may hold values from -0.625 to 0.625
- local_skeleton: bfloat16 [992, 16, 64], P(('groups', 'seg')), parts along dimension 0, may hold values from -6 to 6
- upper_skeleton: bfloat16 [24, 16, 64], P('groups'), parts along dimension 0, may hold values from -6 to 6
- near_offsets: int32 [512, 8], P(('groups', 'seg')), parts along dimension 0, may hold values from -8 to 8, as said below
- local_coupling: int32 [992, 4], P(('groups', 'seg')), parts along dimension 0, may hold values from -4 to 4, as said below
- upper_coupling: int32 [24, 4], P('groups'), parts along dimension 0, may hold values from -4 to 4, as said below
Outputs:
- products: float32 [32, 262144], P(None, ('groups', 'seg')), parts along dimension 1
There are 2 independent parts, one for each index of `groups`. A program takes and returns all parts, laid end to end along the dimension named above; each array names one. Nothing has to cross between parts.
Inputs may be any that keep to these rules, and one draw needn't show every extreme that they name: `near_offsets`: each row holds 8 distinct offsets, the first of them 0. `local_coupling`: each row holds 4 distinct offsets, none of -1, 0, 1. `upper_coupling`: each row holds 4 distinct offsets, none of -1, 0, 1.
All inputs are finite; a program needn't handle non-finite values.
Results may differ from a plain program's by a relative error of at most 0.012.
Values may be sent and summed in bfloat16 or wider, within the bound.
A program may use at most 64 MiB of HBM per device.

v0:
```python
import jax
import jax.numpy as jnp
from jax import lax
from jax.sharding import PartitionSpec as P

REACH = 8


FAR_OFFSETS = (-4, -3, -2, 2, 3, 4)


def with_halo(cells, sides, width):
    for axis, dim in sides:
        count = lax.axis_size(axis)
        ends = count - 1
        head = lax.slice_in_dim(cells, 0, width, axis=dim)
        tail = lax.slice_in_dim(cells, cells.shape[dim] - width, cells.shape[dim], axis=dim)
        cells = jnp.concatenate(
            [
                lax.ppermute(tail, axis, [(i, (i + 1) % count) for i in range(ends)]),
                cells,
                lax.ppermute(head, axis, [((i + 1) % count, i) for i in range(ends)]),
            ],
            axis=dim,
        )
    return cells


def passed_along(x, axis, by):
    peers = lax.axis_size(axis)
    pairs = [(i, i + by) for i in range(peers) if 0 <= i + by < peers]
    return lax.ppermute(x, axis, pairs)


def kernel_tiles(targets, sources, inverse_len):
    target_scaled = (targets.astype(jnp.float32) * inverse_len[:, None]).astype(jnp.bfloat16)
    source_scaled = (sources.astype(jnp.float32) * inverse_len[:, None]).astype(jnp.bfloat16)
    target_wide = target_scaled.astype(jnp.float32)
    source_wide = source_scaled.astype(jnp.float32)
    target_norm = jnp.sum(target_wide * target_wide, axis=-2)
    source_norm = jnp.sum(source_wide * source_wide, axis=-2)
    inner = jnp.einsum(
        "...dm,...dk->...mk", target_scaled, source_scaled, preferred_element_type=jnp.float32
    )
    return jnp.exp(-0.5 * (target_norm[..., :, None] + source_norm[..., None, :] - 2.0 * inner))


def pick_row(array, position):
    return lax.dynamic_index_in_dim(array, position, 0, keepdims=False)


def body(
    points,
    vectors,
    lengthscale,
    leaf_basis,
    local_transfer,
    upper_transfer,
    local_skeleton,
    upper_skeleton,
    near_offsets,
    local_coupling,
    upper_coupling,
):
    inverse_len = 1.0 / lengthscale
    dims = points.shape[0]
    probes = vectors.shape[0]
    leaf_dev, rank_size, leaf_size = leaf_basis.shape
    leaf_levels = leaf_dev.bit_length() - 1
    segments = lax.axis_size("seg")
    seg_levels = segments.bit_length() - 1
    top_cross = seg_levels - 2
    device = lax.axis_index("seg")
    stacked = jnp.concatenate([points, vectors], axis=0)
    widened = with_halo(stacked, (("seg", 1),), REACH * leaf_size)
    source_blocks = widened.reshape(dims + probes, leaf_dev + 2 * REACH, leaf_size)
    own_blocks = points.reshape(dims, leaf_dev, leaf_size)

    def near_leaf(index):
        chosen = index + REACH + near_offsets[index]
        picked = jnp.take(source_blocks, chosen, axis=1)
        source_points = jnp.swapaxes(picked[:dims], 0, 1)
        target_points = lax.dynamic_index_in_dim(own_blocks, index, 1, keepdims=False)
        kernel = kernel_tiles(target_points[None], source_points, inverse_len).astype(jnp.bfloat16)
        return jnp.einsum("mij,pmj->pi", kernel, picked[dims:], preferred_element_type=jnp.float32)

    near_part = lax.map(near_leaf, jnp.arange(leaf_dev, dtype=jnp.int32))
    vector_blocks = vectors.reshape(probes, leaf_dev, leaf_size)
    level_coefs = [
        jnp.einsum(
            "trl,ptl->trp", leaf_basis, vector_blocks, preferred_element_type=jnp.float32
        ).astype(jnp.bfloat16)
    ]
    for height in range(leaf_levels):
        boxes = leaf_dev >> height
        first_row = 2 * leaf_dev - 2 * boxes
        transfer = local_transfer[first_row : first_row + boxes]
        terms = jnp.einsum(
            "trs,trp->tsp", transfer, level_coefs[-1], preferred_element_type=jnp.float32
        )
        paired = terms.reshape(boxes // 2, 2, rank_size, probes)
        level_coefs.append((paired[:, 0] + paired[:, 1]).astype(jnp.bfloat16))
    local_fields = []
    for height in range(leaf_levels + 1):
        boxes = leaf_dev >> height
        first_row = 2 * leaf_dev - 2 * boxes
        skeleton = local_skeleton[first_row : first_row + boxes]
        partner_list = local_coupling[first_row : first_row + boxes]
        packed = jnp.concatenate(
            [level_coefs[height].reshape(boxes, -1), skeleton.reshape(boxes, -1)], axis=1
        )
        reach_devices = -(-4 // boxes)
        moves = [m for m in range(reach_devices, -reach_devices - 1, -1) if m != 0]
        arrived = dict(((m, passed_along(packed, "seg", m)) for m in moves))
        ordered = (
            [arrived[m] for m in range(reach_devices, 0, -1)]
            + [packed]
            + [arrived[-m] for m in range(1, reach_devices + 1)]
        )
        rows_all = jnp.concatenate(ordered, axis=0)
        base = reach_devices * boxes
        coef_all = rows_all[:, : rank_size * probes].reshape(-1, rank_size, probes)
        skel_all = rows_all[:, rank_size * probes :].reshape(-1, dims, rank_size)
        field = jnp.zeros((boxes, rank_size, probes), jnp.float32)
        for offset in FAR_OFFSETS:
            partner_coefs = coef_all[base + offset : base + offset + boxes]
            partner_skel = skel_all[base + offset : base + offset + boxes]
            kernel = kernel_tiles(skeleton, partner_skel, inverse_len).astype(jnp.bfloat16)
            product = jnp.einsum(
                "tij,tjp->tip", kernel, partner_coefs, preferred_element_type=jnp.float32
            )
            weight = jnp.sum((partner_list == offset).astype(jnp.float32), axis=1)
            field = field + weight[:, None, None] * product
        local_fields.append(field)
    cross_coefs = [level_coefs[leaf_levels][0]]
    roots = lax.all_gather(level_coefs[leaf_levels], "seg", axis=0, tiled=True)
    every_level = [roots]
    for above in range(top_cross):
        boxes = segments >> above
        first_row = 2 * segments - 2 * boxes
        transfer = upper_transfer[first_row : first_row + boxes]
        terms = jnp.einsum(
            "trs,trp->tsp", transfer, every_level[-1], preferred_element_type=jnp.float32
        )
        paired = terms.reshape(boxes // 2, 2, rank_size, probes)
        every_level.append((paired[:, 0] + paired[:, 1]).astype(jnp.bfloat16))
    for above in range(1, top_cross + 1):
        cross_coefs.append(pick_row(every_level[above], device // (1 << above)))
    cross_fields = {}
    for above in range(1, top_cross + 1):
        position = device // (1 << above)
        first_row = segments - (segments >> above - 1)
        skeleton = pick_row(upper_skeleton, first_row + position)
        partner_list = pick_row(upper_coupling, first_row + position)
        padded_level = jnp.pad(every_level[above], ((4, 4), (0, 0), (0, 0)))
        field = jnp.zeros((rank_size, probes), jnp.float32)
        for offset in FAR_OFFSETS:
            if abs(offset) * (1 << above) < segments:
                partner_coefs = pick_row(padded_level, position + 4 + offset)
                partner_skel = pick_row(upper_skeleton, first_row + position + offset)
                kernel = kernel_tiles(skeleton, partner_skel, inverse_len).astype(jnp.bfloat16)
                product = jnp.dot(kernel, partner_coefs, preferred_element_type=jnp.float32)
                weight = jnp.sum((partner_list == offset).astype(jnp.float32))
                field = field + weight * product
        cross_fields[above] = field
    field = cross_fields[top_cross]
    for above in range(top_cross, 0, -1):
        child = above - 1
        position = device // (1 << child)
        first_row = 2 * segments - 2 * (segments >> child)
        transfer = pick_row(upper_transfer, first_row + position)
        spread = jnp.dot(transfer, field.astype(jnp.bfloat16), preferred_element_type=jnp.float32)
        if child > 0:
            field = cross_fields[child] + spread
        else:
            field = local_fields[leaf_levels][0] + spread
    level_field = field[None]
    for height in range(leaf_levels - 1, -1, -1):
        boxes = leaf_dev >> height
        first_row = 2 * leaf_dev - 2 * boxes
        transfer = local_transfer[first_row : first_row + boxes]
        spread = jnp.repeat(level_field.astype(jnp.bfloat16), 2, axis=0)
        level_field = local_fields[height] + jnp.einsum(
            "trs,tsp->trp", transfer, spread, preferred_element_type=jnp.float32
        )
    far_part = jnp.einsum(
        "trl,trp->tpl",
        leaf_basis,
        level_field.astype(jnp.bfloat16),
        preferred_element_type=jnp.float32,
    )
    summed = near_part + far_part
    return summed.transpose(1, 0, 2).reshape(probes, leaf_dev * leaf_size)


def solution(mesh):
    in_specs = (
        P(None, ("groups", "seg")),
        P(None, ("groups", "seg")),
        P("groups"),
        P(("groups", "seg"), None, None),
        P(("groups", "seg"), None, None),
        P("groups", None, None),
        P(("groups", "seg"), None, None),
        P("groups", None, None),
        P(("groups", "seg"), None),
        P(("groups", "seg"), None),
        P("groups", None),
    )
    out_specs = P(None, ("groups", "seg"))
    return jax.shard_map(body, mesh=mesh, in_specs=in_specs, out_specs=out_specs, check_vma=False)
```

profile of v0, /device:TPU:5, one launch (start us, length us, event | category | flops | bytes accessed | tf_op | source)
XLA Modules:
  0.0 317.6 jit_solution(1199700698270536949)
XLA Ops:
  0.0 1.2 copy-done
  1.2 1.4 convolution_convert_fusion
  3.3 2.6 collective-permute-start.3
  5.9 3.9 %collective-permute-start.2 = (bf16[16,3072]{1,0:T(8,128)(2,1)S(1)}, bf16[16,3072]{1,0:T(8,128)(2,1)}, u32[]{:S(2)}, u32[]{:S(2)}) collective-permute-start(bf16[16,3072]{1,0:T(8,128)(2,1)S(1)} %constant_dynamic-update-slice_fusion.2), channel_id=1, source_target_pairs={{0,1},{1,2},{2,3},{3,4},{4,5},{5,6},{6,7},{7,8},{8,9},{9,10},{10,1... | collective-permute-start | bytes 294920 | tf_op jit(solution)/shard_map/ppermute | solution.py:32
  12.9 1.9 collective-permute-start.13
  14.8 1.3 collective-permute-start.17
  16.1 4.6 %collective-permute-start.12 = (bf16[1,3072]{1,0:T(2,128)(2,1)}, bf16[1,3072]{1,0:T(2,128)(2,1)}, u32[]{:S(2)}, u32[]{:S(2)}) collective-permute-start(bf16[1,3072]{1,0:T(2,128)(2,1)} %constant_dynamic-update-slice_fusion.10), channel_id=1, source_target_pairs={{0,4},{1,5},{2,6},{3,7},{4,8},{5,9},{6,10},{7,11},{8,12},{9,13},{1... | collective-permute-start | bytes 18440 | tf_op jit(solution)/shard_map/ppermute | solution.py:32
  20.7 20.5 %all-gather = bf16[16,1,64,32]{2,3,1,0:T(8,128)(2,1)S(1)} all-gather(bf16[1,1,64,32]{2,3,1,0:T(8,128)(2,1)S(1)} %fusion.506), channel_id=2, replica_groups=mesh['groups'=2,'seg'=16] {'seg'}, dimensions={0}, use_global_device_ids=true | all-gather | bytes 69632 | tf_op jit(solution)/shard_map/all_gather | solution.py:136
  46.7 1.1 fusion.317
  56.3 1.1 fusion.285
  63.1 1.9 collective-permute-start.14
  66.5 3.4 %collective-permute-start.15 = (bf16[1,3072]{1,0:T(2,128)(2,1)}, bf16[1,3072]{1,0:T(2,128)(2,1)S(1)}, u32[]{:S(2)}, u32[]{:S(2)}) collective-permute-start(bf16[1,3072]{1,0:T(2,128)(2,1)} %constant_dynamic-update-slice_fusion.10), channel_id=1, source_target_pairs={{2,0},{3,1},{4,2},{5,3},{6,4},{7,5},{8,6},{9,7},{10,8},{11,9},{12,... | collective-permute-start | bytes 18440 | tf_op jit(solution)/shard_map/ppermute | solution.py:32
  70.5 1.9 collective-permute-start.16
  73.2 1.9 collective-permute-start.11
  75.1 2.0 collective-permute-start.10
  77.6 4.4 %collective-permute-start.9 = (bf16[2,3072]{1,0:T(2,128)(2,1)S(1)}, bf16[2,3072]{1,0:T(2,128)(2,1)S(1)}, u32[]{:S(2)}, u32[]{:S(2)}) collective-permute-start(bf16[2,3072]{1,0:T(2,128)(2,1)S(1)} %constant_dynamic-update-slice_fusion.8), channel_id=1, source_target_pairs={{0,1},{1,2},{2,3},{3,4},{4,5},{5,6},{6,7},{7,8},{8,9},{9,10},{10,1... | collective-permute-start | bytes 36872 | tf_op jit(solution)/shard_map/ppermute | solution.py:32
  93.0 4.0 %collective-permute-start.8 = (bf16[2,3072]{1,0:T(2,128)(2,1)S(1)}, bf16[2,3072]{1,0:T(2,128)(2,1)S(1)}, u32[]{:S(2)}, u32[]{:S(2)}) collective-permute-start(bf16[2,3072]{1,0:T(2,128)(2,1)S(1)} %constant_dynamic-update-slice_fusion.8), channel_id=1, source_target_pairs={{0,2},{1,3},{2,4},{3,5},{4,6},{5,7},{6,8},{7,9},{8,10},{9,11},{10,... | collective-permute-start | bytes 36872 | tf_op jit(solution)/shard_map/ppermute | solution.py:32
  97.0 1.9 collective-permute-start.7
  99.1 4.5 %collective-permute-start.6 = (bf16[4,3072]{1,0:T(4,128)(2,1)S(1)}, bf16[4,3072]{1,0:T(4,128)(2,1)S(1)}, u32[]{:S(2)}, u32[]{:S(2)}) collective-permute-start(bf16[4,3072]{1,0:T(4,128)(2,1)S(1)} %constant_dynamic-update-slice_fusion.6), channel_id=1, source_target_pairs={{0,1},{1,2},{2,3},{3,4},{4,5},{5,6},{6,7},{7,8},{8,9},{9,10},{10,1... | collective-permute-start | bytes 73736 | tf_op jit(solution)/shard_map/ppermute | solution.py:32
  103.7 1.9 collective-permute-start.5
  109.9 4.5 %collective-permute-start.4 = (bf16[8,3072]{1,0:T(8,128)(2,1)S(1)}, bf16[8,3072]{1,0:T(8,128)(2,1)S(1)}, u32[]{:S(2)}, u32[]{:S(2)}) collective-permute-start(bf16[8,3072]{1,0:T(8,128)(2,1)S(1)} %constant_dynamic-update-slice_fusion.4), channel_id=1, source_target_pairs={{0,1},{1,2},{2,3},{3,4},{4,5},{5,6},{6,7},{7,8},{8,9},{9,10},{10,1... | collective-permute-start | bytes 147464 | tf_op jit(solution)/shard_map/ppermute | solution.py:32
  114.5 1.9 collective-permute-start.1
  121.0 1.9 convolution_multiply_fusion.27
  122.8 1.9 convolution_multiply_fusion.28
  124.7 1.3 fusion.168
  126.1 1.9 fusion.166
  128.0 1.3 fusion.165
  129.3 1.3 fusion.169
  131.4 4.7 %collective-permute-start = (bf16[48,4096]{1,0:T(8,128)(2,1)}, bf16[48,4096]{1,0:T(8,128)(2,1)}, u32[]{:S(2)}, u32[]{:S(2)}) collective-permute-start(bf16[48,4096]{1,0:T(8,128)(2,1)} %get-tuple-element.179), channel_id=1, source_target_pairs={{0,1},{1,2},{2,3},{3,4},{4,5},{5,6},{6,7},{7,8},{8,9},{9,10},{10,1... | collective-permute-start | bytes 1179656 | tf_op jit(solution)/shard_map/ppermute | solution.py:20
  139.9 1.1 fusion.105
  141.0 2.1 fusion.109
  143.1 2.1 fusion.111
  145.2 1.5 fusion.119
  147.2 2.0 fusion.144
  149.3 1.7 pad_maximum_fusion.1
  151.8 1.5 fusion.442
  154.7 1.8 slice.527
  156.5 1.8 slice.530
  159.1 1.7 slice.536
  162.0 1.4 fusion.76
  163.4 2.5 fusion.75
  165.9 2.5 fusion.73
  168.4 2.4 fusion.71
  170.8 1.6 fusion.69
  172.4 1.4 fusion.67
  173.8 1.1 pad_maximum_fusion
  175.1 139.6 %while.10 = (s32[]{:T(128)}, f32[16,32,512]{2,1,0:T(8,128)}, s32[16]{0:T(128)S(1)}, s32[16,8]{1,0:T(8,128)S(1)}, bf16[48,32,512]{2,0,1:T(8,128)(2,1)S(1)}, /*ind...) while((s32[]{:T(128)}, f32[16,32,512]{2,1,0:T(8,128)}, ...), condition=%wide.region_3.4_spmd, body=%wide.region_0.3_spmd.sunk | while | flops 212669024 | bytes 2237947 | solution.py:87
  179.7 4.1 %fusion.906 = f32[16,32,512]{2,1,0:T(8,128)} fusion(f32[16,32,512]{2,1,0:T(8,128)} %get-tuple-element.306, s32[]{:T(128)S(6)} %copy.238, f32[8,512]{1,0:T(8,128)S(1)} %multiply_reduce_fusion.51, f32[512]{0:T(512)S(1)} %multiply_reduce_fusion.52, bf16[48,8,512]{2,0,1:T(8,128)(2,1)S(1)} %select_bitcast_fusion.2, f32[16]{0:T(128)S(1)} %get-tuple-element.322, ...), kind=kOutput, calls=%fused_computation.8.clone.1 | convolution fusion | flops 212033536 | bytes 494600 | tf_op jit(solution)/shard_map/while/body/eval_jaxpr/mij,pmj->pi/dot_general | solution.py:85
  188.4 4.1 %fusion.906 = f32[16,32,512]{2,1,0:T(8,128)} fusion(f32[16,32,512]{2,1,0:T(8,128)} %get-tuple-element.306, s32[]{:T(128)S(6)} %copy.238, f32[8,512]{1,0:T(8,128)S(1)} %multiply_reduce_fusion.51, f32[512]{0:T(512)S(1)} %multiply_reduce_fusion.52, bf16[48,8,512]{2,0,1:T(8,128)(2,1)S(1)} %select_bitcast_fusion.2, f32[16]{0:T(128)S(1)} %get-tuple-element.322, ...), kind=kOutput, calls=%fused_computation.8.clone.1 | convolution fusion | flops 212033536 | bytes 494600 | tf_op jit(solution)/shard_map/while/body/eval_jaxpr/mij,pmj->pi/dot_general | solution.py:85
  197.1 4.2 %fusion.906 = f32[16,32,512]{2,1,0:T(8,128)} fusion(f32[16,32,512]{2,1,0:T(8,128)} %get-tuple-element.306, s32[]{:T(128)S(6)} %copy.238, f32[8,512]{1,0:T(8,128)S(1)} %multiply_reduce_fusion.51, f32[512]{0:T(512)S(1)} %multiply_reduce_fusion.52, bf16[48,8,512]{2,0,1:T(8,128)(2,1)S(1)} %select_bitcast_fusion.2, f32[16]{0:T(128)S(1)} %get-tuple-element.322, ...), kind=kOutput, calls=%fused_computation.8.clone.1 | convolution fusion | flops 212033536 | bytes 494600 | tf_op jit(solution)/shard_map/while/body/eval_jaxpr/mij,pmj->pi/dot_general | solution.py:85
  205.9 4.2 %fusion.906 = f32[16,32,512]{2,1,0:T(8,128)} fusion(f32[16,32,512]{2,1,0:T(8,128)} %get-tuple-element.306, s32[]{:T(128)S(6)} %copy.238, f32[8,512]{1,0:T(8,128)S(1)} %multiply_reduce_fusion.51, f32[512]{0:T(512)S(1)} %multiply_reduce_fusion.52, bf16[48,8,512]{2,0,1:T(8,128)(2,1)S(1)} %select_bitcast_fusion.2, f32[16]{0:T(128)S(1)} %get-tuple-element.322, ...), kind=kOutput, calls=%fused_computation.8.clone.1 | convolution fusion | flops 212033536 | bytes 494600 | tf_op jit(solution)/shard_map/while/body/eval_jaxpr/mij,pmj->pi/dot_general | solution.py:85
  214.6 4.2 %fusion.906 = f32[16,32,512]{2,1,0:T(8,128)} fusion(f32[16,32,512]{2,1,0:T(8,128)} %get-tuple-element.306, s32[]{:T(128)S(6)} %copy.238, f32[8,512]{1,0:T(8,128)S(1)} %multiply_reduce_fusion.51, f32[512]{0:T(512)S(1)} %multiply_reduce_fusion.52, bf16[48,8,512]{2,0,1:T(8,128)(2,1)S(1)} %select_bitcast_fusion.2, f32[16]{0:T(128)S(1)} %get-tuple-element.322, ...), kind=kOutput, calls=%fused_computation.8.clone.1 | convolution fusion | flops 212033536 | bytes 494600 | tf_op jit(solution)/shard_map/while/body/eval_jaxpr/mij,pmj->pi/dot_general | solution.py:85
  223.3 4.2 %fusion.906 = f32[16,32,512]{2,1,0:T(8,128)} fusion(f32[16,32,512]{2,1,0:T(8,128)} %get-tuple-element.306, s32[]{:T(128)S(6)} %copy.238, f32[8,512]{1,0:T(8,128)S(1)} %multiply_reduce_fusion.51, f32[512]{0:T(512)S(1)} %multiply_reduce_fusion.52, bf16[48,8,512]{2,0,1:T(8,128)(2,1)S(1)} %select_bitcast_fusion.2, f32[16]{0:T(128)S(1)} %get-tuple-element.322, ...), kind=kOutput, calls=%fused_computation.8.clone.1 | convolution fusion | flops 212033536 | bytes 494600 | tf_op jit(solution)/shard_map/while/body/eval_jaxpr/mij,pmj->pi/dot_general | solution.py:85
  232.0 4.2 %fusion.906 = f32[16,32,512]{2,1,0:T(8,128)} fusion(f32[16,32,512]{2,1,0:T(8,128)} %get-tuple-element.306, s32[]{:T(128)S(6)} %copy.238, f32[8,512]{1,0:T(8,128)S(1)} %multiply_reduce_fusion.51, f32[512]{0:T(512)S(1)} %multiply_reduce_fusion.52, bf16[48,8,512]{2,0,1:T(8,128)(2,1)S(1)} %select_bitcast_fusion.2, f32[16]{0:T(128)S(1)} %get-tuple-element.322, ...), kind=kOutput, calls=%fused_computation.8.clone.1 | convolution fusion | flops 212033536 | bytes 494600 | tf_op jit(solution)/shard_map/while/body/eval_jaxpr/mij,pmj->pi/dot_general | solution.py:85
  240.8 4.2 %fusion.906 = f32[16,32,512]{2,1,0:T(8,128)} fusion(f32[16,32,512]{2,1,0:T(8,128)} %get-tuple-element.306, s32[]{:T(128)S(6)} %copy.238, f32[8,512]{1,0:T(8,128)S(1)} %multiply_reduce_fusion.51, f32[512]{0:T(512)S(1)} %multiply_reduce_fusion.52, bf16[48,8,512]{2,0,1:T(8,128)(2,1)S(1)} %select_bitcast_fusion.2, f32[16]{0:T(128)S(1)} %get-tuple-element.322, ...), kind=kOutput, calls=%fused_computation.8.clone.1 | convolution fusion | flops 212033536 | bytes 494600 | tf_op jit(solution)/shard_map/while/body/eval_jaxpr/mij,pmj->pi/dot_general | solution.py:85
  249.5 4.2 %fusion.906 = f32[16,32,512]{2,1,0:T(8,128)} fusion(f32[16,32,512]{2,1,0:T(8,128)} %get-tuple-element.306, s32[]{:T(128)S(6)} %copy.238, f32[8,512]{1,0:T(8,128)S(1)} %multiply_reduce_fusion.51, f32[512]{0:T(512)S(1)} %multiply_reduce_fusion.52, bf16[48,8,512]{2,0,1:T(8,128)(2,1)S(1)} %select_bitcast_fusion.2, f32[16]{0:T(128)S(1)} %get-tuple-element.322, ...), kind=kOutput, calls=%fused_computation.8.clone.1 | convolution fusion | flops 212033536 | bytes 494600 | tf_op jit(solution)/shard_map/while/body/eval_jaxpr/mij,pmj->pi/dot_general | solution.py:85
  258.2 4.2 %fusion.906 = f32[16,32,512]{2,1,0:T(8,128)} fusion(f32[16,32,512]{2,1,0:T(8,128)} %get-tuple-element.306, s32[]{:T(128)S(6)} %copy.238, f32[8,512]{1,0:T(8,128)S(1)} %multiply_reduce_fusion.51, f32[512]{0:T(512)S(1)} %multiply_reduce_fusion.52, bf16[48,8,512]{2,0,1:T(8,128)(2,1)S(1)} %select_bitcast_fusion.2, f32[16]{0:T(128)S(1)} %get-tuple-element.322, ...), kind=kOutput, calls=%fused_computation.8.clone.1 | convolution fusion | flops 212033536 | bytes 494600 | tf_op jit(solution)/shard_map/while/body/eval_jaxpr/mij,pmj->pi/dot_general | solution.py:85
  266.9 4.2 %fusion.906 = f32[16,32,512]{2,1,0:T(8,128)} fusion(f32[16,32,512]{2,1,0:T(8,128)} %get-tuple-element.306, s32[]{:T(128)S(6)} %copy.238, f32[8,512]{1,0:T(8,128)S(1)} %multiply_reduce_fusion.51, f32[512]{0:T(512)S(1)} %multiply_reduce_fusion.52, bf16[48,8,512]{2,0,1:T(8,128)(2,1)S(1)} %select_bitcast_fusion.2, f32[16]{0:T(128)S(1)} %get-tuple-element.322, ...), kind=kOutput, calls=%fused_computation.8.clone.1 | convolution fusion | flops 212033536 | bytes 494600 | tf_op jit(solution)/shard_map/while/body/eval_jaxpr/mij,pmj->pi/dot_general | solution.py:85
  275.7 4.2 %fusion.906 = f32[16,32,512]{2,1,0:T(8,128)} fusion(f32[16,32,512]{2,1,0:T(8,128)} %get-tuple-element.306, s32[]{:T(128)S(6)} %copy.238, f32[8,512]{1,0:T(8,128)S(1)} %multiply_reduce_fusion.51, f32[512]{0:T(512)S(1)} %multiply_reduce_fusion.52, bf16[48,8,512]{2,0,1:T(8,128)(2,1)S(1)} %select_bitcast_fusion.2, f32[16]{0:T(128)S(1)} %get-tuple-element.322, ...), kind=kOutput, calls=%fused_computation.8.clone.1 | convolution fusion | flops 212033536 | bytes 494600 | tf_op jit(solution)/shard_map/while/body/eval_jaxpr/mij,pmj->pi/dot_general | solution.py:85
  284.4 4.2 %fusion.906 = f32[16,32,512]{2,1,0:T(8,128)} fusion(f32[16,32,512]{2,1,0:T(8,128)} %get-tuple-element.306, s32[]{:T(128)S(6)} %copy.238, f32[8,512]{1,0:T(8,128)S(1)} %multiply_reduce_fusion.51, f32[512]{0:T(512)S(1)} %multiply_reduce_fusion.52, bf16[48,8,512]{2,0,1:T(8,128)(2,1)S(1)} %select_bitcast_fusion.2, f32[16]{0:T(128)S(1)} %get-tuple-element.322, ...), kind=kOutput, calls=%fused_computation.8.clone.1 | convolution fusion | flops 212033536 | bytes 494600 | tf_op jit(solution)/shard_map/while/body/eval_jaxpr/mij,pmj->pi/dot_general | solution.py:85
  293.1 4.2 %fusion.906 = f32[16,32,512]{2,1,0:T(8,128)} fusion(f32[16,32,512]{2,1,0:T(8,128)} %get-tuple-element.306, s32[]{:T(128)S(6)} %copy.238, f32[8,512]{1,0:T(8,128)S(1)} %multiply_reduce_fusion.51, f32[512]{0:T(512)S(1)} %multiply_reduce_fusion.52, bf16[48,8,512]{2,0,1:T(8,128)(2,1)S(1)} %select_bitcast_fusion.2, f32[16]{0:T(128)S(1)} %get-tuple-element.322, ...), kind=kOutput, calls=%fused_computation.8.clone.1 | convolution fusion | flops 212033536 | bytes 494600 | tf_op jit(solution)/shard_map/while/body/eval_jaxpr/mij,pmj->pi/dot_general | solution.py:85
  301.8 4.2 %fusion.906 = f32[16,32,512]{2,1,0:T(8,128)} fusion(f32[16,32,512]{2,1,0:T(8,128)} %get-tuple-element.306, s32[]{:T(128)S(6)} %copy.238, f32[8,512]{1,0:T(8,128)S(1)} %multiply_reduce_fusion.51, f32[512]{0:T(512)S(1)} %multiply_reduce_fusion.52, bf16[48,8,512]{2,0,1:T(8,128)(2,1)S(1)} %select_bitcast_fusion.2, f32[16]{0:T(128)S(1)} %get-tuple-element.322, ...), kind=kOutput, calls=%fused_computation.8.clone.1 | convolution fusion | flops 212033536 | bytes 494600 | tf_op jit(solution)/shard_map/while/body/eval_jaxpr/mij,pmj->pi/dot_general | solution.py:85
  310.6 4.2 %fusion.906 = f32[16,32,512]{2,1,0:T(8,128)} fusion(f32[16,32,512]{2,1,0:T(8,128)} %get-tuple-element.306, s32[]{:T(128)S(6)} %copy.238, f32[8,512]{1,0:T(8,128)S(1)} %multiply_reduce_fusion.51, f32[512]{0:T(512)S(1)} %multiply_reduce_fusion.52, bf16[48,8,512]{2,0,1:T(8,128)(2,1)S(1)} %select_bitcast_fusion.2, f32[16]{0:T(128)S(1)} %get-tuple-element.322, ...), kind=kOutput, calls=%fused_computation.8.clone.1 | convolution fusion | flops 212033536 | bytes 494600 | tf_op jit(solution)/shard_map/while/body/eval_jaxpr/mij,pmj->pi/dot_general | solution.py:85
  314.7 1.8 fusion.34
  (416 shorter events, 92.6 us)
Async XLA Ops:
  0.0 1.2 copy-start
  0.0 3.1 slice-start
  0.0 9.8 %copy-start.1 = (bf16[30,64,64]{2,1,0:T(8,128)(2,1)S(1)}, bf16[30,64,64]{2,1,0:T(8,128)(2,1)}, u32[]{:S(2)}) copy-start(bf16[30,64,64]{2,1,0:T(8,128)(2,1)} %param.17) | copy-start | bytes 737284
  3.3 146.0 %collective-permute-start.3 = (bf16[16,3072]{1,0:T(8,128)(2,1)S(1)}, bf16[16,3072]{1,0:T(8,128)(2,1)S(1)}, u32[]{:S(2)}, u32[]{:S(2)}) collective-permute-start(bf16[16,3072]{1,0:T(8,128)(2,1)S(1)} %constant_dynamic-update-slice_fusion.2), channel_id=1, source_target_pairs={{1,0},{2,1},{3,2},{4,3},{5,4},{6,5},{7,6},{8,7},{9,8},{10,9},{11,1... | collective-permute-start | bytes 294920 | tf_op jit(solution)/shard_map/ppermute | solution.py:32
  5.9 143.4 %collective-permute-start.2 = (bf16[16,3072]{1,0:T(8,128)(2,1)S(1)}, bf16[16,3072]{1,0:T(8,128)(2,1)}, u32[]{:S(2)}, u32[]{:S(2)}) collective-permute-start(bf16[16,3072]{1,0:T(8,128)(2,1)S(1)} %constant_dynamic-update-slice_fusion.2), channel_id=1, source_target_pairs={{0,1},{1,2},{2,3},{3,4},{4,5},{5,6},{6,7},{7,8},{8,9},{9,10},{10,1... | collective-permute-start | bytes 294920 | tf_op jit(solution)/shard_map/ppermute | solution.py:32
  10.1 2.1 slice-start.1
  10.3 30.9 %copy-start.11 = (s32[31,4]{0,1:T(4,128)S(1)}, s32[31,4]{0,1:T(4,128)}, u32[]{:S(2)}) copy-start(s32[31,4]{0,1:T(4,128)} %param.22) | copy-start | bytes 1492
  10.3 35.3 %copy-start.2 = (bf16[16,8192]{1,0:T(8,128)(2,1)S(1)}, bf16[16,8192]{1,0:T(8,128)(2,1)}, u32[]{:S(2)}) copy-start(bf16[16,8192]{1,0:T(8,128)(2,1)} %param.13) | copy-start | bytes 786436
  10.5 35.1 %copy-start.4 = (bf16[32,8192]{1,0:T(8,128)(2,1)S(1)}, bf16[32,8192]{1,0:T(8,128)(2,1)}, u32[]{:S(2)}) copy-start(bf16[32,8192]{1,0:T(8,128)(2,1)} %param.14) | copy-start | bytes 1572868
  12.9 50.2 %collective-permute-start.13 = (bf16[1,3072]{1,0:T(2,128)(2,1)}, bf16[1,3072]{1,0:T(2,128)(2,1)}, u32[]{:S(2)}, u32[]{:S(2)}) collective-permute-start(bf16[1,3072]{1,0:T(2,128)(2,1)} %constant_dynamic-update-slice_fusion.10), channel_id=1, source_target_pairs={{0,3},{1,4},{2,5},{3,6},{4,7},{5,8},{6,9},{7,10},{8,11},{9,12},{10... | collective-permute-start | bytes 18440 | tf_op jit(solution)/shard_map/ppermute | solution.py:32
  14.8 51.6 %collective-permute-start.17 = (bf16[1,3072]{1,0:T(2,128)(2,1)}, bf16[1,3072]{1,0:T(2,128)(2,1)}, u32[]{:S(2)}, u32[]{:S(2)}) collective-permute-start(bf16[1,3072]{1,0:T(2,128)(2,1)} %constant_dynamic-update-slice_fusion.10), channel_id=1, source_target_pairs={{4,0},{5,1},{6,2},{7,3},{8,4},{9,5},{10,6},{11,7},{12,8},{13,9},{1... | collective-permute-start | bytes 18440 | tf_op jit(solution)/shard_map/ppermute | solution.py:32
  16.1 54.4 %collective-permute-start.12 = (bf16[1,3072]{1,0:T(2,128)(2,1)}, bf16[1,3072]{1,0:T(2,128)(2,1)}, u32[]{:S(2)}, u32[]{:S(2)}) collective-permute-start(bf16[1,3072]{1,0:T(2,128)(2,1)} %constant_dynamic-update-slice_fusion.10), channel_id=1, source_target_pairs={{0,4},{1,5},{2,6},{3,7},{4,8},{5,9},{6,10},{7,11},{8,12},{9,13},{1... | collective-permute-start | bytes 18440 | tf_op jit(solution)/shard_map/ppermute | solution.py:32
  45.6 1.1 copy-start.37
  45.7 3.3 %copy-start.13 = (bf16[2,2048]{1,0:T(2,128)(2,1)S(1)}, bf16[2,2048]{1,0:T(2,128)(2,1)}, u32[]{:S(2)}) copy-start(bf16[2,2048]{1,0:T(2,128)(2,1)} %convert_element_type.1681) | copy-start | bytes 24580
  45.7 3.3 %slice-start.2 = ((bf16[31,16,64]{2,1,0:T(8,128)(2,1)}), bf16[2,16,64]{2,1,0:T(8,128)(2,1)S(1)}, s32[]{:S(2)}) async-start(bf16[31,16,64]{2,1,0:T(8,128)(2,1)} %param.19), calls=%async_computation.2 | async-start | bytes 16384 | tf_op jit(solution)/shard_map/slice | solution.py:107
  45.7 3.4 %slice-start.3 = ((bf16[31,16,64]{2,1,0:T(8,128)(2,1)}), bf16[4,16,64]{2,1,0:T(8,128)(2,1)S(1)}, s32[]{:S(2)}) async-start(bf16[31,16,64]{2,1,0:T(8,128)(2,1)} %param.19), calls=%async_computation.3 | async-start | bytes 32768 | tf_op jit(solution)/shard_map/slice | solution.py:107
  45.7 3.5 %slice-start.4 = ((bf16[31,16,64]{2,1,0:T(8,128)(2,1)}), bf16[8,16,64]{2,1,0:T(8,128)(2,1)S(1)}, s32[]{:S(2)}) async-start(bf16[31,16,64]{2,1,0:T(8,128)(2,1)} %param.19), calls=%async_computation.4 | async-start | bytes 65536 | tf_op jit(solution)/shard_map/slice | solution.py:107
  45.7 3.7 %copy-start.14 = (s32[12,4]{0,1:T(4,128)S(1)}, s32[12,4]{0,1:T(4,128)}, u32[]{:S(2)}) copy-start(s32[12,4]{0,1:T(4,128)} %param.23) | copy-start | bytes 580
  45.7 4.5 %copy-start.12 = (bf16[12,16,64]{2,1,0:T(8,128)(2,1)S(1)}, bf16[12,16,64]{2,1,0:T(8,128)(2,1)}, u32[]{:S(2)}) copy-start(bf16[12,16,64]{2,1,0:T(8,128)(2,1)} %param.20) | copy-start | bytes 73732
  47.8 14.5 %copy-start.15 = (s32[16,8]{0,1:T(8,128)S(1)}, s32[16,8]{0,1:T(8,128)}, u32[]{:S(2)}) copy-start(s32[16,8]{0,1:T(8,128)} %param.21) | copy-start | bytes 1540
  49.3 37.3 %copy-start.3 = (bf16[31,16,64]{2,1,0:T(8,128)(2,1)S(1)}, bf16[31,16,64]{2,1,0:T(8,128)(2,1)}, u32[]{:S(2)}) copy-start(bf16[31,16,64]{2,1,0:T(8,128)(2,1)} %param.19) | copy-start | bytes 190468
  61.4 45.3 %copy-start.36 = (f32[2]{0:T(128)S(1)}, f32[2]{0:T(128)}, u32[]{:S(2)}) copy-start(f32[2]{0:T(128)} %get-tuple-element.106) | copy-start | bytes 28
  62.4 44.7 %copy-start.35 = (f32[2]{0:T(128)S(1)}, f32[2]{0:T(128)}, u32[]{:S(2)}) copy-start(f32[2]{0:T(128)} %get-tuple-element.105) | copy-start | bytes 28
  63.1 44.4 %copy-start.34 = (f32[2]{0:T(128)S(1)}, f32[2]{0:T(128)}, u32[]{:S(2)}) copy-start(f32[2]{0:T(128)} %get-tuple-element.104) | copy-start | bytes 28
  63.1 44.8 %copy-start.33 = (f32[2]{0:T(128)S(1)}, f32[2]{0:T(128)}, u32[]{:S(2)}) copy-start(f32[2]{0:T(128)} %get-tuple-element.103) | copy-start | bytes 28
  63.1 10.1 %collective-permute-start.14 = (bf16[1,3072]{1,0:T(2,128)(2,1)}, bf16[1,3072]{1,0:T(2,128)(2,1)S(1)}, u32[]{:S(2)}, u32[]{:S(2)}) collective-permute-start(bf16[1,3072]{1,0:T(2,128)(2,1)} %constant_dynamic-update-slice_fusion.10), channel_id=1, source_target_pairs={{0,2},{1,3},{2,4},{3,5},{4,6},{5,7},{6,8},{7,9},{8,10},{9,11},{10,... | collective-permute-start | bytes 18440 | tf_op jit(solution)/shard_map/ppermute | solution.py:32
  66.5 8.7 %collective-permute-start.15 = (bf16[1,3072]{1,0:T(2,128)(2,1)}, bf16[1,3072]{1,0:T(2,128)(2,1)S(1)}, u32[]{:S(2)}, u32[]{:S(2)}) collective-permute-start(bf16[1,3072]{1,0:T(2,128)(2,1)} %constant_dynamic-update-slice_fusion.10), channel_id=1, source_target_pairs={{2,0},{3,1},{4,2},{5,3},{6,4},{7,5},{8,6},{9,7},{10,8},{11,9},{12,... | collective-permute-start | bytes 18440 | tf_op jit(solution)/shard_map/ppermute | solution.py:32
  70.5 7.1 %collective-permute-start.16 = (bf16[1,3072]{1,0:T(2,128)(2,1)}, bf16[1,3072]{1,0:T(2,128)(2,1)S(1)}, u32[]{:S(2)}, u32[]{:S(2)}) collective-permute-start(bf16[1,3072]{1,0:T(2,128)(2,1)} %constant_dynamic-update-slice_fusion.10), channel_id=1, source_target_pairs={{3,0},{4,1},{5,2},{6,3},{7,4},{8,5},{9,6},{10,7},{11,8},{12,9},{13... | collective-permute-start | bytes 18440 | tf_op jit(solution)/shard_map/ppermute | solution.py:32
  73.2 19.8 %collective-permute-start.11 = (bf16[2,3072]{1,0:T(2,128)(2,1)S(1)}, bf16[2,3072]{1,0:T(2,128)(2,1)S(1)}, u32[]{:S(2)}, u32[]{:S(2)}) collective-permute-start(bf16[2,3072]{1,0:T(2,128)(2,1)S(1)} %constant_dynamic-update-slice_fusion.8), channel_id=1, source_target_pairs={{2,0},{3,1},{4,2},{5,3},{6,4},{7,5},{8,6},{9,7},{10,8},{11,9},{12,... | collective-permute-start | bytes 36872 | tf_op jit(solution)/shard_map/ppermute | solution.py:32
  75.1 21.8 %collective-permute-start.10 = (bf16[2,3072]{1,0:T(2,128)(2,1)S(1)}, bf16[2,3072]{1,0:T(2,128)(2,1)S(1)}, u32[]{:S(2)}, u32[]{:S(2)}) collective-permute-start(bf16[2,3072]{1,0:T(2,128)(2,1)S(1)} %constant_dynamic-update-slice_fusion.8), channel_id=1, source_target_pairs={{1,0},{2,1},{3,2},{4,3},{5,4},{6,5},{7,6},{8,7},{9,8},{10,9},{11,1... | collective-permute-start | bytes 36872 | tf_op jit(solution)/shard_map/ppermute | solution.py:32
  77.6 21.5 %collective-permute-start.9 = (bf16[2,3072]{1,0:T(2,128)(2,1)S(1)}, bf16[2,3072]{1,0:T(2,128)(2,1)S(1)}, u32[]{:S(2)}, u32[]{:S(2)}) collective-permute-start(bf16[2,3072]{1,0:T(2,128)(2,1)S(1)} %constant_dynamic-update-slice_fusion.8), channel_id=1, source_target_pairs={{0,1},{1,2},{2,3},{3,4},{4,5},{5,6},{6,7},{7,8},{8,9},{9,10},{10,1... | collective-permute-start | bytes 36872 | tf_op jit(solution)/shard_map/ppermute | solution.py:32
  82.2 26.2 %copy-start.16 = (f32[2]{0:T(128)S(1)}, f32[2]{0:T(128)}, u32[]{:S(2)}) copy-start(f32[2]{0:T(128)} %get-tuple-element.107) | copy-start | bytes 28
  85.0 23.7 %copy-start.32 = (f32[2]{0:T(128)S(1)}, f32[2]{0:T(128)}, u32[]{:S(2)}) copy-start(f32[2]{0:T(128)} %get-tuple-element.102) | copy-start | bytes 28
  93.0 10.7 %collective-permute-start.8 = (bf16[2,3072]{1,0:T(2,128)(2,1)S(1)}, bf16[2,3072]{1,0:T(2,128)(2,1)S(1)}, u32[]{:S(2)}, u32[]{:S(2)}) collective-permute-start(bf16[2,3072]{1,0:T(2,128)(2,1)S(1)} %constant_dynamic-update-slice_fusion.8), channel_id=1, source_target_pairs={{0,2},{1,3},{2,4},{3,5},{4,6},{5,7},{6,8},{7,9},{8,10},{9,11},{10,... | collective-permute-start | bytes 36872 | tf_op jit(solution)/shard_map/ppermute | solution.py:32
  97.0 13.0 %collective-permute-start.7 = (bf16[4,3072]{1,0:T(4,128)(2,1)S(1)}, bf16[4,3072]{1,0:T(4,128)(2,1)S(1)}, u32[]{:S(2)}, u32[]{:S(2)}) collective-permute-start(bf16[4,3072]{1,0:T(4,128)(2,1)S(1)} %constant_dynamic-update-slice_fusion.6), channel_id=1, source_target_pairs={{1,0},{2,1},{3,2},{4,3},{5,4},{6,5},{7,6},{8,7},{9,8},{10,9},{11,1... | collective-permute-start | bytes 73736 | tf_op jit(solution)/shard_map/ppermute | solution.py:32
  99.1 15.3 %collective-permute-start.6 = (bf16[4,3072]{1,0:T(4,128)(2,1)S(1)}, bf16[4,3072]{1,0:T(4,128)(2,1)S(1)}, u32[]{:S(2)}, u32[]{:S(2)}) collective-permute-start(bf16[4,3072]{1,0:T(4,128)(2,1)S(1)} %constant_dynamic-update-slice_fusion.6), channel_id=1, source_target_pairs={{0,1},{1,2},{2,3},{3,4},{4,5},{5,6},{6,7},{7,8},{8,9},{9,10},{10,1... | collective-permute-start | bytes 73736 | tf_op jit(solution)/shard_map/ppermute | solution.py:32
  103.7 27.7 %collective-permute-start.5 = (bf16[8,3072]{1,0:T(8,128)(2,1)S(1)}, bf16[8,3072]{1,0:T(8,128)(2,1)S(1)}, u32[]{:S(2)}, u32[]{:S(2)}) collective-permute-start(bf16[8,3072]{1,0:T(8,128)(2,1)S(1)} %constant_dynamic-update-slice_fusion.4), channel_id=1, source_target_pairs={{1,0},{2,1},{3,2},{4,3},{5,4},{6,5},{7,6},{8,7},{9,8},{10,9},{11,1... | collective-permute-start | bytes 147464 | tf_op jit(solution)/shard_map/ppermute | solution.py:32
  107.9 18.2 %copy-start.31 = (f32[4]{0:T(128)S(1)}, f32[4]{0:T(128)}, u32[]{:S(2)}) copy-start(f32[4]{0:T(128)} %get-tuple-element.99) | copy-start | bytes 52
  108.7 19.3 %copy-start.30 = (f32[4]{0:T(128)S(1)}, f32[4]{0:T(128)}, u32[]{:S(2)}) copy-start(f32[4]{0:T(128)} %get-tuple-element.100) | copy-start | bytes 52
  109.2 20.1 %copy-start.29 = (f32[4]{0:T(128)S(1)}, f32[4]{0:T(128)}, u32[]{:S(2)}) copy-start(f32[4]{0:T(128)} %get-tuple-element.96) | copy-start | bytes 52
  109.9 26.2 %collective-permute-start.4 = (bf16[8,3072]{1,0:T(8,128)(2,1)S(1)}, bf16[8,3072]{1,0:T(8,128)(2,1)S(1)}, u32[]{:S(2)}, u32[]{:S(2)}) collective-permute-start(bf16[8,3072]{1,0:T(8,128)(2,1)S(1)} %constant_dynamic-update-slice_fusion.4), channel_id=1, source_target_pairs={{0,1},{1,2},{2,3},{3,4},{4,5},{5,6},{6,7},{7,8},{8,9},{9,10},{10,1... | collective-permute-start | bytes 147464 | tf_op jit(solution)/shard_map/ppermute | solution.py:32
  114.5 59.3 %collective-permute-start.1 = (bf16[48,4096]{1,0:T(8,128)(2,1)}, bf16[48,4096]{1,0:T(8,128)(2,1)S(1)}, u32[]{:S(2)}, u32[]{:S(2)}) collective-permute-start(bf16[48,4096]{1,0:T(8,128)(2,1)} %get-tuple-element.180), channel_id=1, source_target_pairs={{1,0},{2,1},{3,2},{4,3},{5,4},{6,5},{7,6},{8,7},{9,8},{10,9},{11,1... | collective-permute-start | bytes 1179656 | tf_op jit(solution)/shard_map/ppermute | solution.py:22
  130.6 9.3 %copy-start.28 = (f32[8]{0:T(128)S(1)}, f32[8]{0:T(128)}, u32[]{:S(2)}) copy-start(f32[8]{0:T(128)} %get-tuple-element.94) | copy-start | bytes 100
  131.4 42.4 %collective-permute-start = (bf16[48,4096]{1,0:T(8,128)(2,1)}, bf16[48,4096]{1,0:T(8,128)(2,1)}, u32[]{:S(2)}, u32[]{:S(2)}) collective-permute-start(bf16[48,4096]{1,0:T(8,128)(2,1)} %get-tuple-element.179), channel_id=1, source_target_pairs={{0,1},{1,2},{2,3},{3,4},{4,5},{5,6},{6,7},{7,8},{8,9},{9,10},{10,1... | collective-permute-start | bytes 1179656 | tf_op jit(solution)/shard_map/ppermute | solution.py:20
  136.3 4.8 %copy-start.27 = (f32[8]{0:T(128)S(1)}, f32[8]{0:T(128)}, u32[]{:S(2)}) copy-start(f32[8]{0:T(128)} %get-tuple-element.92) | copy-start | bytes 100
  136.5 6.6 %copy-start.26 = (f32[8]{0:T(128)S(1)}, f32[8]{0:T(128)}, u32[]{:S(2)}) copy-start(f32[8]{0:T(128)} %get-tuple-element.91) | copy-start | bytes 100
  136.9 8.3 %copy-start.25 = (f32[8]{0:T(128)S(1)}, f32[8]{0:T(128)}, u32[]{:S(2)}) copy-start(f32[8]{0:T(128)} %get-tuple-element.95) | copy-start | bytes 100
  139.4 7.3 %copy-start.24 = (f32[8]{0:T(128)S(1)}, f32[8]{0:T(128)}, u32[]{:S(2)}) copy-start(f32[8]{0:T(128)} %get-tuple-element.93) | copy-start | bytes 100
  139.8 7.4 %copy-start.23 = (f32[8]{0:T(128)S(1)}, f32[8]{0:T(128)}, u32[]{:S(2)}) copy-start(f32[8]{0:T(128)} %get-tuple-element.90) | copy-start | bytes 100
  141.0 5.7 %copy-start.38 = (f32[8,64,32]{1,2,0:T(8,128)S(1)}, f32[8,64,32]{1,2,0:T(8,128)}, u32[]{:S(2)}) copy-start(f32[8,64,32]{1,2,0:T(8,128)} %fusion.105) | copy-start | bytes 196612
  153.3 4.9 %copy-start.9 = (bf16[16,2048]{1,0:T(8,128)(2,1)S(1)}, bf16[16,2048]{1,0:T(8,128)(2,1)}, u32[]{:S(2)}) copy-start(bf16[16,2048]{1,0:T(8,128)(2,1)} %get-tuple-element.184) | copy-start | bytes 196612
  153.3 7.5 %copy-start.8 = (bf16[16,2048]{1,0:T(8,128)(2,1)S(1)}, bf16[16,2048]{1,0:T(8,128)(2,1)}, u32[]{:S(2)}) copy-start(bf16[16,2048]{1,0:T(8,128)(2,1)} %get-tuple-element.183) | copy-start | bytes 196612
  153.6 8.4 %copy-start.5 = (bf16[16,64,32]{2,1,0:T(8,128)(2,1)S(1)}, bf16[16,64,32]{2,1,0:T(8,128)(2,1)}, u32[]{:S(2)}) copy-start(bf16[16,64,32]{2,1,0:T(8,128)(2,1)} %slice.524) | copy-start | bytes 196612
  153.6 8.4 %copy-start.22 = (f32[16]{0:T(128)S(1)}, f32[16]{0:T(128)}, u32[]{:S(2)}) copy-start(f32[16]{0:T(128)} %get-tuple-element.129) | copy-start | bytes 196
  158.2 5.2 %copy-start.21 = (f32[16]{0:T(128)S(1)}, f32[16]{0:T(128)}, u32[]{:S(2)}) copy-start(f32[16]{0:T(128)} %get-tuple-element.125) | copy-start | bytes 196
  161.7 4.2 %copy-start.20 = (f32[16]{0:T(128)S(1)}, f32[16]{0:T(128)}, u32[]{:S(2)}) copy-start(f32[16]{0:T(128)} %get-tuple-element.126) | copy-start | bytes 196
  162.0 6.3 %copy-start.19 = (f32[16]{0:T(128)S(1)}, f32[16]{0:T(128)}, u32[]{:S(2)}) copy-start(f32[16]{0:T(128)} %get-tuple-element.127) | copy-start | bytes 196
  163.4 7.3 %copy-start.7 = (bf16[16,64,32]{2,1,0:T(8,128)(2,1)S(1)}, bf16[16,64,32]{2,1,0:T(8,128)(2,1)}, u32[]{:S(2)}) copy-start(bf16[16,64,32]{2,1,0:T(8,128)(2,1)} %slice.536) | copy-start | bytes 196612
  163.4 7.3 %copy-start.18 = (f32[16]{0:T(128)S(1)}, f32[16]{0:T(128)}, u32[]{:S(2)}) copy-start(f32[16]{0:T(128)} %get-tuple-element.128) | copy-start | bytes 196
  165.9 6.5 %copy-start.6 = (bf16[16,64,32]{2,1,0:T(8,128)(2,1)S(1)}, bf16[16,64,32]{2,1,0:T(8,128)(2,1)}, u32[]{:S(2)}) copy-start(bf16[16,64,32]{2,1,0:T(8,128)(2,1)} %slice.539) | copy-start | bytes 196612
  165.9 6.5 %copy-start.17 = (f32[16]{0:T(128)S(1)}, f32[16]{0:T(128)}, u32[]{:S(2)}) copy-start(f32[16]{0:T(128)} %get-tuple-element.124) | copy-start | bytes 196
  175.1 139.6 %copy-start.10 = (bf16[8,64,32]{1,2,0:T(8,128)(2,1)S(1)}, bf16[8,64,32]{1,2,0:T(8,128)(2,1)}, u32[]{:S(2)}) copy-start(bf16[8,64,32]{1,2,0:T(8,128)(2,1)} %fusion.144) | copy-start | bytes 98308
where the time goes:
time: 322 us; the launch traced here: 318 us
  matrix products  125 us (39%)
  starting transfers between devices  53.3 us (17%)
  local copies, waits for them, and re-layouts  48.7 us (15%)
  loops' own time  37.4 us (12%)
  other arithmetic  31.2 us (10%)
  blocking collectives  20.5 us (6%)
    dot_general x16, matrix products, near_leaf(): jnp.einsum('mij,pmj->pi', kernel, picked[dims:], preferred_element_type=j...  66.4 us
    ppermute x16, starting transfers between devices, passed_along(): return lax.ppermute(x, axis, pairs)  46.7 us
    dot_general x30, matrix products, body(): jnp.einsum('tij,tjp->tip', kernel, partner_coefs, preferred_element_type=...  39 us
    another operation x1, loops' own time, body(): near_part = lax.map(near_leaf, jnp.arange(leaf_dev, dtype=jnp.int32))  37.4 us
    all_gather x1, blocking collectives, body(): roots = lax.all_gather(level_coefs[leaf_levels], 'seg', axis=0, tiled=True)  20.5 us
    slice x30, local copies, waits for them, and re-layouts, body(): partner_coefs = coef_all[base + offset:base + offset + boxes]  17.4 us
    reduce_sum x16, other arithmetic, kernel_tiles(): target_norm = jnp.sum(target_wide * target_wide, axis=-2)  13 us
    dot_general x10, matrix products, body(): product = jnp.dot(kernel, partner_coefs, preferred_element_type=jnp.float32)  10.2 us
  transfers between devices with their start and end apart: 18, of which 0 were waited for; matrix products, arithmetic and copies ran while one was open for 30% of the time, Pallas kernels for 0%

commit v1 on v0

--- a/solution.py
+++ b/solution.py
@@ -1,12 +1,83 @@
+import functools
+
 import jax
 import jax.numpy as jnp
 from jax import lax
+from jax.experimental import pallas as pl
+from jax.experimental.pallas import tpu as pltpu
 from jax.sharding import PartitionSpec as P
 
 REACH = 8
 
 
 FAR_OFFSETS = (-4, -3, -2, 2, 3, 4)
+
+
+LOG2E = 1.4426950408889634
+
+
+def split3(x):
+    a = x.astype(jnp.bfloat16); r = x - a.astype(jnp.float32)
+    b = r.astype(jnp.bfloat16); r = r - b.astype(jnp.float32)
+    return a, b, r.astype(jnp.bfloat16)
+
+
+def augment(points, inv):
+    s = (points.astype(jnp.float32) * inv).astype(jnp.bfloat16)
+    w = s.astype(jnp.float32)
+    t1, t2, t3 = split3(w * LOG2E)
+    n = (-0.5 * LOG2E) * jnp.sum(w * w, axis=-2, keepdims=True)
+    n1, n2, n3 = (x.astype(jnp.float32) for x in split3(n))
+    row = lax.broadcasted_iota(jnp.int32, w.shape, w.ndim - 2)
+    nr = jnp.where(row % 3 == 0, n1, jnp.where(row % 3 == 1, n2, n3))
+    src_n = jnp.where(row < 3, nr, jnp.where(row < 6, 1.0, 0.0)).astype(jnp.bfloat16)
+    tgt_n = jnp.where(row < 3, 1.0, jnp.where(row < 6, nr, 0.0)).astype(jnp.bfloat16)
+    return (jnp.concatenate([s, s, s, src_n], axis=-2), jnp.concatenate([t1, t2, t3, tgt_n], axis=-2))
+
+
+def near_kernel(reach, leaf, dims, off_ref, inv_ref, wide_ref, out_ref, src, tgt):
+    leaf_dev, near = off_ref.shape
+    rows = wide_ref.shape[0]
+    inv = inv_ref[...]
+    blocks = wide_ref.shape[1] // leaf
+
+    def prep(b, _):
+        col = pl.ds(pl.multiple_of(b * leaf, leaf), leaf)
+        s, t = augment(wide_ref[0:dims, col], inv)
+        src[col, :] = s.T
+        tgt[:, col] = t
+        return 0
+
+    lax.fori_loop(0, blocks, prep, 0)
+
+    def one(t, _):
+        own = pl.ds(pl.multiple_of((t + reach) * leaf, leaf), leaf)
+        acc = None
+        target = tgt[:, own]
+        for m in range(near):
+            c = t + reach + off_ref[t, m]
+            col = pl.ds(pl.multiple_of(c * leaf, leaf), leaf)
+            k = jnp.exp2(jnp.dot(src[col, :], target, preferred_element_type=jnp.float32))
+            d = jnp.dot(wide_ref[dims:rows, col], k.astype(jnp.bfloat16), preferred_element_type=jnp.float32)
+            acc = d if acc is None else acc + d
+        out_ref[:, pl.ds(pl.multiple_of(t * leaf, leaf), leaf)] = acc
+        return 0
+
+    lax.fori_loop(0, leaf_dev, one, 0)
+
+
+def near_product(offsets, inverse_len, widened, leaf, dims):
+    leaf_dev = offsets.shape[0]
+    width = widened.shape[1]
+    depth = 4 * dims
+    return pl.pallas_call(
+        functools.partial(near_kernel, REACH, leaf, dims),
+        in_specs=[pl.BlockSpec(memory_space=pltpu.SMEM)] + [pl.BlockSpec(memory_space=pltpu.VMEM)] * 2,
+        out_specs=pl.BlockSpec(memory_space=pltpu.VMEM),
+        out_shape=jax.ShapeDtypeStruct((widened.shape[0] - dims, leaf_dev * leaf), jnp.float32),
+        scratch_shapes=[pltpu.VMEM((width, depth), jnp.bfloat16), pltpu.VMEM((depth, width), jnp.bfloat16)],
+        compiler_params=pltpu.CompilerParams(vmem_limit_bytes=40 << 20),
+    )(offsets, inverse_len[:, None], widened)
 
 
 def with_halo(cells, sides, width):
@@ -73,18 +144,7 @@
     device = lax.axis_index("seg")
     stacked = jnp.concatenate([points, vectors], axis=0)
     widened = with_halo(stacked, (("seg", 1),), REACH * leaf_size)
-    source_blocks = widened.reshape(dims + probes, leaf_dev + 2 * REACH, leaf_size)
-    own_blocks = points.reshape(dims, leaf_dev, leaf_size)
-
-    def near_leaf(index):
-        chosen = index + REACH + near_offsets[index]
-        picked = jnp.take(source_blocks, chosen, axis=1)
-        source_points = jnp.swapaxes(picked[:dims], 0, 1)
-        target_points = lax.dynamic_index_in_dim(own_blocks, index, 1, keepdims=False)
-        kernel = kernel_tiles(target_points[None], source_points, inverse_len).astype(jnp.bfloat16)
-        return jnp.einsum("mij,pmj->pi", kernel, picked[dims:], preferred_element_type=jnp.float32)
-
-    near_part = lax.map(near_leaf, jnp.arange(leaf_dev, dtype=jnp.int32))
+    near_part = near_product(near_offsets, inverse_len, widened, leaf_size, dims)
     vector_blocks = vectors.reshape(probes, leaf_dev, leaf_size)
     level_coefs = [
         jnp.einsum(
@@ -189,8 +249,7 @@
         level_field.astype(jnp.bfloat16),
         preferred_element_type=jnp.float32,
     )
-    summed = near_part + far_part
-    return summed.transpose(1, 0, 2).reshape(probes, leaf_dev * leaf_size)
+    return near_part + far_part.transpose(1, 0, 2).reshape(probes, leaf_dev * leaf_size)
 
 
 def solution(mesh):

time: 322 us -> 230 us (0.71)
  matrix products: 125 us -> 61.7 us
  Pallas kernels: 0 us -> 45.2 us
  loops' own time: 37.4 us -> 0 us
  local copies, waits for them, and re-layouts: 48.7 us -> 29.5 us
  other arithmetic: 31.2 us -> 16.1 us
    dot_general x16 -> x0, matrix products: 66.4 us -> none  [near_leaf(): jnp.einsum('mij,pmj->pi', kernel, picked[dims:], preferred_element_type=j...]
    pallas_call x0 -> x1, Pallas kernels: none -> 45.2 us  [near_product(): pl.pallas_call(functools.partial(near_kernel, REACH, leaf, dims), in_spec...]
    another operation x1 -> x0, loops' own time: 37.4 us -> none  [body(): near_part = lax.map(near_leaf, jnp.arange(leaf_dev, dtype=jnp.int32))]
    reduce_sum x16 -> x0, other arithmetic: 13 us -> none  [kernel_tiles(): target_norm = jnp.sum(target_wide * target_wide, axis=-2)]
    dynamic_slice x16 -> x0, local copies, waits for them, and re-layouts: 9.41 us -> none  [body(): near_part = lax.map(near_leaf, jnp.arange(leaf_dev, dtype=jnp.int32))]
    gather x16 -> x0, local copies, waits for them, and re-layouts: 9.16 us -> none  [near_leaf(): picked = jnp.take(source_blocks, chosen, axis=1)]
    dot_general x10, matrix products: 10.2 us -> 15 us  [body(): product = jnp.dot(kernel, partner_coefs, preferred_element_type=jnp.float32)]
  transfers between devices with their start and end apart: 18 -> 18, of which waited for: 0 -> 0; matrix products, arithmetic and copies ran while one was open for 30% -> 45% of each run, Pallas kernels for 0% -> 0%
where the time goes in v1:
time: 230 us; the launch traced here: 228 us
  matrix products  61.7 us (27%)
  starting transfers between devices  53.3 us (23%)
  Pallas kernels  45.2 us (20%)
  local copies, waits for them, and re-layouts  29.5 us (13%)
  blocking collectives  20.5 us (9%)
  other arithmetic  16.1 us (7%)
    ppermute x16, starting transfers between devices, passed_along(): return lax.ppermute(x, axis, pairs)  46.7 us
    pallas_call x1, Pallas kernels, near_product(): pl.pallas_call(functools.partial(near_kernel, REACH, leaf, dims), in_spec...  45.2 us
    dot_general x30, matrix products, body(): jnp.einsum('tij,tjp->tip', kernel, partner_coefs, preferred_element_type=...  40.8 us
    all_gather x1, blocking collectives, body(): roots = lax.all_gather(level_coefs[leaf_levels], 'seg', axis=0, tiled=True)  20.5 us
    slice x30, local copies, waits for them, and re-layouts, body(): partner_coefs = coef_all[base + offset:base + offset + boxes]  15.5 us
    dot_general x10, matrix products, body(): product = jnp.dot(kernel, partner_coefs, preferred_element_type=jnp.float32)  15 us
    convert_element_type x17, other arithmetic, kernel_tiles(): sources.astype(jnp.float32) * inverse_len[:, None]  5.01 us
    ppermute x1, starting transfers between devices, with_halo(): lax.ppermute(tail, axis, [(i, (i + 1) % count) for i in range(ends)])  4.71 us
  transfers between devices with their start and end apart: 18, of which 0 were waited for; matrix products, arithmetic and copies ran while one was open for 45% of the time, Pallas kernels for 0%

profile of v1, /device:TPU:5, one launch (start us, length us, event | category | flops | bytes accessed | tf_op | source)
XLA Modules:
  0.0 227.5 jit_solution(14553759224205226034)
XLA Ops:
  0.0 1.2 copy-done
  1.2 1.4 convolution_convert_fusion
  3.3 2.6 %collective-permute-start.3 = (bf16[16,3072]{1,0:T(8,128)(2,1)S(1)}, bf16[16,3072]{1,0:T(8,128)(2,1)S(1)}, u32[]{:S(2)}, u32[]{:S(2)}) collective-permute-start(bf16[16,3072]{1,0:T(8,128)(2,1)S(1)} %constant_dynamic-update-slice_fusion.2), channel_id=1, source_target_pairs={{1,0},{2,1},{3,2},{4,3},{5,4},{6,5},{7,6},{8,7},{9,8},{10,9},{11,1... | collective-permute-start | bytes 294920 | tf_op jit(solution)/shard_map/ppermute | solution.py:103
  5.9 3.9 %collective-permute-start.2 = (bf16[16,3072]{1,0:T(8,128)(2,1)S(1)}, bf16[16,3072]{1,0:T(8,128)(2,1)S(1)}, u32[]{:S(2)}, u32[]{:S(2)}) collective-permute-start(bf16[16,3072]{1,0:T(8,128)(2,1)S(1)} %constant_dynamic-update-slice_fusion.2), channel_id=1, source_target_pairs={{0,1},{1,2},{2,3},{3,4},{4,5},{5,6},{6,7},{7,8},{8,9},{9,10},{10,1... | collective-permute-start | bytes 294920 | tf_op jit(solution)/shard_map/ppermute | solution.py:103
  12.9 1.9 collective-permute-start.13
  14.8 1.3 collective-permute-start.17
  16.1 4.6 %collective-permute-start.12 = (bf16[1,3072]{1,0:T(2,128)(2,1)}, bf16[1,3072]{1,0:T(2,128)(2,1)}, u32[]{:S(2)}, u32[]{:S(2)}) collective-permute-start(bf16[1,3072]{1,0:T(2,128)(2,1)} %constant_dynamic-update-slice_fusion.10), channel_id=1, source_target_pairs={{0,4},{1,5},{2,6},{3,7},{4,8},{5,9},{6,10},{7,11},{8,12},{9,13},{1... | collective-permute-start | bytes 18440 | tf_op jit(solution)/shard_map/ppermute | solution.py:103
  21.2 20.5 %all-gather = bf16[16,1,64,32]{2,3,1,0:T(8,128)(2,1)S(1)} all-gather(bf16[1,1,64,32]{2,3,1,0:T(8,128)(2,1)S(1)} %fusion.471), channel_id=2, replica_groups=mesh['groups'=2,'seg'=16] {'seg'}, dimensions={0}, use_global_device_ids=true | all-gather | bytes 69632 | tf_op jit(solution)/shard_map/all_gather | solution.py:196
  45.6 1.1 constant_dynamic-update-slice_fusion
  50.4 0.9 multiply_reduce_fusion.33
  51.4 1.7 fusion.234
  53.1 1.7 fusion.232
  54.8 1.8 fusion.229
  56.5 1.7 fusion.273
  58.4 1.7 fusion.252
  60.1 1.8 fusion.250
  61.9 1.8 fusion.247
  63.7 1.0 fusion.244
  64.6 1.0 fusion.241
  65.6 0.9 fusion.272
  68.1 1.9 collective-permute-start.14
  71.5 3.4 %collective-permute-start.15 = (bf16[1,3072]{1,0:T(2,128)(2,1)}, bf16[1,3072]{1,0:T(2,128)(2,1)S(1)}, u32[]{:S(2)}, u32[]{:S(2)}) collective-permute-start(bf16[1,3072]{1,0:T(2,128)(2,1)} %constant_dynamic-update-slice_fusion.10), channel_id=1, source_target_pairs={{2,0},{3,1},{4,2},{5,3},{6,4},{7,5},{8,6},{9,7},{10,8},{11,9},{12,... | collective-permute-start | bytes 18440 | tf_op jit(solution)/shard_map/ppermute | solution.py:103
  75.5 1.9 collective-permute-start.16
  78.2 1.9 collective-permute-start.11
  80.1 2.0 collective-permute-start.10
  82.6 4.4 %collective-permute-start.9 = (bf16[2,3072]{1,0:T(2,128)(2,1)}, bf16[2,3072]{1,0:T(2,128)(2,1)S(1)}, u32[]{:S(2)}, u32[]{:S(2)}) collective-permute-start(bf16[2,3072]{1,0:T(2,128)(2,1)} %constant_dynamic-update-slice_fusion.8), channel_id=1, source_target_pairs={{0,1},{1,2},{2,3},{3,4},{4,5},{5,6},{6,7},{7,8},{8,9},{9,10},{10,1... | collective-permute-start | bytes 36872 | tf_op jit(solution)/shard_map/ppermute | solution.py:103
  91.8 1.0 fusion.267
  92.7 1.0 fusion.270
  93.7 1.1 fusion.265
  94.8 1.0 fusion.262
  95.8 1.0 fusion.259
  96.8 1.1 fusion.271
  98.0 4.0 %collective-permute-start.8 = (bf16[2,3072]{1,0:T(2,128)(2,1)}, bf16[2,3072]{1,0:T(2,128)(2,1)S(1)}, u32[]{:S(2)}, u32[]{:S(2)}) collective-permute-start(bf16[2,3072]{1,0:T(2,128)(2,1)} %constant_dynamic-update-slice_fusion.8), channel_id=1, source_target_pairs={{0,2},{1,3},{2,4},{3,5},{4,6},{5,7},{6,8},{7,9},{8,10},{9,11},{10,... | collective-permute-start | bytes 36872 | tf_op jit(solution)/shard_map/ppermute | solution.py:103
  102.0 1.9 collective-permute-start.7
  104.2 4.5 %collective-permute-start.6 = (bf16[4,3072]{1,0:T(4,128)(2,1)S(1)}, bf16[4,3072]{1,0:T(4,128)(2,1)S(1)}, u32[]{:S(2)}, u32[]{:S(2)}) collective-permute-start(bf16[4,3072]{1,0:T(4,128)(2,1)S(1)} %constant_dynamic-update-slice_fusion.6), channel_id=1, source_target_pairs={{0,1},{1,2},{2,3},{3,4},{4,5},{5,6},{6,7},{7,8},{8,9},{9,10},{10,1... | collective-permute-start | bytes 73736 | tf_op jit(solution)/shard_map/ppermute | solution.py:103
  108.7 1.9 collective-permute-start.5
  111.7 1.0 fusion.146
  112.7 1.1 fusion.148
  116.3 4.5 %collective-permute-start.4 = (bf16[8,3072]{1,0:T(8,128)(2,1)S(1)}, bf16[8,3072]{1,0:T(8,128)(2,1)S(1)}, u32[]{:S(2)}, u32[]{:S(2)}) collective-permute-start(bf16[8,3072]{1,0:T(8,128)(2,1)S(1)} %constant_dynamic-update-slice_fusion.4), channel_id=1, source_target_pairs={{0,1},{1,2},{2,3},{3,4},{4,5},{5,6},{6,7},{7,8},{8,9},{9,10},{10,1... | collective-permute-start | bytes 147464 | tf_op jit(solution)/shard_map/ppermute | solution.py:103
  120.8 1.9 collective-permute-start.1
  125.5 1.0 convolution_multiply_fusion.27
  126.6 1.3 convolution_multiply_fusion.28
  127.8 1.3 fusion.133
  130.0 1.3 fusion.134
  132.1 4.7 %collective-permute-start = (bf16[48,4096]{1,0:T(8,128)(2,1)}, bf16[48,4096]{1,0:T(8,128)(2,1)}, u32[]{:S(2)}, u32[]{:S(2)}) collective-permute-start(bf16[48,4096]{1,0:T(8,128)(2,1)} %get-tuple-element.92), channel_id=1, source_target_pairs={{0,1},{1,2},{2,3},{3,4},{4,5},{5,6},{6,7},{7,8},{8,9},{9,10},{10,1... | collective-permute-start | bytes 1179656 | tf_op jit(solution)/shard_map/ppermute | solution.py:91
  141.2 1.2 fusion.70
  142.3 2.1 fusion.74
  144.4 2.0 fusion.76
  146.5 2.2 fusion.84
  148.7 1.5 fusion.83
  150.1 2.0 fusion.109
  156.8 1.8 slice.521
  158.5 1.8 slice.524
  161.2 1.8 slice.530
  164.1 2.3 %fusion.41 = f32[16,64,32]{1,2,0:T(8,128)} fusion(bf16[16,64,32]{2,1,0:T(8,128)(2,1)} %slice.518, f32[16,64]{1,0:T(8,128)S(1)} %get-tuple-element.86, f32[16,64]{1,0:T(8,128)S(1)} %get-tuple-element.91, f32[16]{0:T(128)S(1)} %copy-done.22, f32[16,16,64]{2,1,0:T(8,128)S(1)} %reshape.1222, f32[16]{0:T(128)S(1)} %copy-done.13, ...), kind=kOutput, calls=%fused_computation.50 | convolution fusion | flops 6733824 | bytes 411136 | tf_op jit(solution)/shard_map/tij,tjp->tip/dot_general | solution.py:189
  166.5 2.4 %fusion.40 = f32[16,64,32]{1,2,0:T(8,128)} fusion(f32[16,64,32]{1,2,0:T(8,128)} %fusion.41, bf16[16,64,32]{2,1,0:T(8,128)(2,1)} %slice.521, f32[16,64]{1,0:T(8,128)S(1)} %get-tuple-element.87, f32[16,64]{1,0:T(8,128)S(1)} %get-tuple-element.91, f32[16]{0:T(128)S(1)} %copy-done.21, f32[16,16,64]{2,1,0:T(8,128)S(1)} %reshape.1223, f32[16]{0:T(128)S(1)} %copy-done.13, ...), kind=kOutput, calls=%fused_computation.49 | convolution fusion | flops 6766592 | bytes 542208 | tf_op jit(solution)/shard_map/tij,tjp->tip/dot_general | solution.py:189
  168.9 2.5 %fusion.38 = f32[16,64,32]{1,2,0:T(8,128)} fusion(f32[16,64,32]{1,2,0:T(8,128)} %fusion.40, bf16[16,64,32]{2,1,0:T(8,128)(2,1)} %slice.524, f32[16,64]{1,0:T(8,128)S(1)} %get-tuple-element.88, f32[16,64]{1,0:T(8,128)S(1)} %get-tuple-element.91, f32[16]{0:T(128)S(1)} %copy-done.20, f32[16,16,64]{2,1,0:T(8,128)S(1)} %reshape.1224, f32[16]{0:T(128)S(1)} %copy-done.13, ...), kind=kOutput, calls=%fused_computation.47 | convolution fusion | flops 6766592 | bytes 542208 | tf_op jit(solution)/shard_map/tij,tjp->tip/dot_general | solution.py:189
  171.3 2.4 %fusion.36 = f32[16,64,32]{1,2,0:T(8,128)} fusion(f32[16,64,32]{1,2,0:T(8,128)} %fusion.38, bf16[16,64,32]{2,1,0:T(8,128)(2,1)} %slice.527, f32[16,64]{1,0:T(8,128)S(1)} %get-tuple-element.89, f32[16,64]{1,0:T(8,128)S(1)} %get-tuple-element.91, f32[16]{0:T(128)S(1)} %copy-done.19, f32[16,16,64]{2,1,0:T(8,128)S(1)} %reshape.1225, f32[16]{0:T(128)S(1)} %copy-done.13, ...), kind=kOutput, calls=%fused_computation.45 | convolution fusion | flops 6766592 | bytes 542208 | tf_op jit(solution)/shard_map/tij,tjp->tip/dot_general | solution.py:189
  173.8 2.4 %fusion.34 = f32[16,64,32]{1,2,0:T(8,128)} fusion(f32[16,64,32]{1,2,0:T(8,128)} %fusion.36, bf16[16,64,32]{2,1,0:T(8,128)(2,1)} %slice.530, f32[16,64]{1,0:T(8,128)S(1)} %get-tuple-element.90, f32[16,64]{1,0:T(8,128)S(1)} %get-tuple-element.91, f32[16]{0:T(128)S(1)} %copy-done.18, f32[16,16,64]{2,1,0:T(8,128)S(1)} %reshape.1226, f32[16]{0:T(128)S(1)} %copy-done.13, ...), kind=kOutput, calls=%fused_computation.43 | convolution fusion | flops 6766592 | bytes 542208 | tf_op jit(solution)/shard_map/tij,tjp->tip/dot_general | solution.py:189
  176.2 2.3 %fusion.32 = f32[16,64,32]{1,2,0:T(8,128)} fusion(f32[16,64,32]{1,2,0:T(8,128)} %fusion.34, bf16[16,64,32]{2,1,0:T(8,128)(2,1)S(1)} %copy-done.4, f32[16,64]{1,0:T(8,128)S(1)} %get-tuple-element.85, f32[16,64]{1,0:T(8,128)S(1)} %get-tuple-element.91, f32[16]{0:T(128)S(1)} %copy-done.17, f32[16,16,64]{2,1,0:T(8,128)S(1)} %reshape.1227, ...), kind=kOutput, calls=%fused_computation.41 | convolution fusion | flops 6766592 | bytes 738816 | tf_op jit(solution)/shard_map/tij,tjp->tip/dot_general | solution.py:189
  178.6 1.4 convolution_bitcast_fusion
  180.1 1.2 pad_maximum_fusion.wide_ref
  181.3 45.2 %shard_map.109 = f32[32,8192]{1,0:T(8,128)S(1)} custom-call(s32[16,8]{1,0:T(8,128)S(1)} %copy.61.off_ref, f32[16,1]{1,0:T(8,128)S(1)} %copy.62.inv_ref, bf16[48,16384]{1,0:T(8,128)(2,1)S(1)} %pad_maximum_fusion.wide_ref), custom_call_target="tpu_custom_call" | custom-call | tf_op jit(solution)/shard_map/pallas_call | solution.py:73
  226.4 1.1 add.1022
  (271 shorter events, 40.3 us)
Async XLA Ops:
  0.0 1.2 copy-start
  0.0 3.1 %slice-start = ((bf16[31,16,64]{2,1,0:T(8,128)(2,1)}), bf16[16,16,64]{2,1,0:T(8,128)(2,1)S(1)}, s32[]{:S(2)}) async-start(bf16[31,16,64]{2,1,0:T(8,128)(2,1)} %param.17), calls=%async_computation | async-start | bytes 131072 | tf_op jit(solution)/shard_map/slice | solution.py:167
  0.0 9.8 %copy-start.1 = (bf16[30,64,64]{2,1,0:T(8,128)(2,1)S(1)}, bf16[30,64,64]{2,1,0:T(8,128)(2,1)}, u32[]{:S(2)}) copy-start(bf16[30,64,64]{2,1,0:T(8,128)(2,1)} %param.15) | copy-start | bytes 737284
  3.3 148.9 %collective-permute-start.3 = (bf16[16,3072]{1,0:T(8,128)(2,1)S(1)}, bf16[16,3072]{1,0:T(8,128)(2,1)S(1)}, u32[]{:S(2)}, u32[]{:S(2)}) collective-permute-start(bf16[16,3072]{1,0:T(8,128)(2,1)S(1)} %constant_dynamic-update-slice_fusion.2), channel_id=1, source_target_pairs={{1,0},{2,1},{3,2},{4,3},{5,4},{6,5},{7,6},{8,7},{9,8},{10,9},{11,1... | collective-permute-start | bytes 294920 | tf_op jit(solution)/shard_map/ppermute | solution.py:103
  5.9 146.3 %collective-permute-start.2 = (bf16[16,3072]{1,0:T(8,128)(2,1)S(1)}, bf16[16,3072]{1,0:T(8,128)(2,1)S(1)}, u32[]{:S(2)}, u32[]{:S(2)}) collective-permute-start(bf16[16,3072]{1,0:T(8,128)(2,1)S(1)} %constant_dynamic-update-slice_fusion.2), channel_id=1, source_target_pairs={{0,1},{1,2},{2,3},{3,4},{4,5},{5,6},{6,7},{7,8},{8,9},{9,10},{10,1... | collective-permute-start | bytes 294920 | tf_op jit(solution)/shard_map/ppermute | solution.py:103
  10.1 2.1 slice-start.1
  10.3 10.4 %copy-start.38 = (f32[16]{0:T(128)S(1)}, f32[16]{0:T(128)}, u32[]{:S(2)}) copy-start(f32[16]{0:T(128)} %param.13) | copy-start | bytes 196
  10.3 31.5 %copy-start.9 = (s32[31,4]{0,1:T(4,128)S(1)}, s32[31,4]{0,1:T(4,128)}, u32[]{:S(2)}) copy-start(s32[31,4]{0,1:T(4,128)} %param.20) | copy-start | bytes 1492
  10.3 35.2 %copy-start.5 = (bf16[16,8192]{1,0:T(8,128)(2,1)S(1)}, bf16[16,8192]{1,0:T(8,128)(2,1)}, u32[]{:S(2)}) copy-start(bf16[16,8192]{1,0:T(8,128)(2,1)} %param.11) | copy-start | bytes 786436
  12.9 55.2 %collective-permute-start.13 = (bf16[1,3072]{1,0:T(2,128)(2,1)}, bf16[1,3072]{1,0:T(2,128)(2,1)}, u32[]{:S(2)}, u32[]{:S(2)}) collective-permute-start(bf16[1,3072]{1,0:T(2,128)(2,1)} %constant_dynamic-update-slice_fusion.10), channel_id=1, source_target_pairs={{0,3},{1,4},{2,5},{3,6},{4,7},{5,8},{6,9},{7,10},{8,11},{9,12},{10... | collective-permute-start | bytes 18440 | tf_op jit(solution)/shard_map/ppermute | solution.py:103
  14.8 56.6 %collective-permute-start.17 = (bf16[1,3072]{1,0:T(2,128)(2,1)}, bf16[1,3072]{1,0:T(2,128)(2,1)}, u32[]{:S(2)}, u32[]{:S(2)}) collective-permute-start(bf16[1,3072]{1,0:T(2,128)(2,1)} %constant_dynamic-update-slice_fusion.10), channel_id=1, source_target_pairs={{4,0},{5,1},{6,2},{7,3},{8,4},{9,5},{10,6},{11,7},{12,8},{13,9},{1... | collective-permute-start | bytes 18440 | tf_op jit(solution)/shard_map/ppermute | solution.py:103
  16.1 59.4 %collective-permute-start.12 = (bf16[1,3072]{1,0:T(2,128)(2,1)}, bf16[1,3072]{1,0:T(2,128)(2,1)}, u32[]{:S(2)}, u32[]{:S(2)}) collective-permute-start(bf16[1,3072]{1,0:T(2,128)(2,1)} %constant_dynamic-update-slice_fusion.10), channel_id=1, source_target_pairs={{0,4},{1,5},{2,6},{3,7},{4,8},{5,9},{6,10},{7,11},{8,12},{9,13},{1... | collective-permute-start | bytes 18440 | tf_op jit(solution)/shard_map/ppermute | solution.py:103
  21.2 93.8 %copy-start.11 = (f32[16]{0:T(128)}, f32[16]{0:T(128)S(1)}, u32[]{:S(2)}) copy-start(f32[16]{0:T(128)S(1)} %broadcast_divide_fusion) | copy-start | bytes 196
  45.6 2.1 copy-start.3
  46.7 2.6 %slice-start.2 = ((bf16[31,16,64]{2,1,0:T(8,128)(2,1)}), bf16[2,16,64]{2,1,0:T(8,128)(2,1)S(1)}, s32[]{:S(2)}) async-start(bf16[31,16,64]{2,1,0:T(8,128)(2,1)} %param.17), calls=%async_computation.2 | async-start | bytes 16384 | tf_op jit(solution)/shard_map/slice | solution.py:167
  46.7 2.7 %slice-start.3 = ((bf16[31,16,64]{2,1,0:T(8,128)(2,1)}), bf16[4,16,64]{2,1,0:T(8,128)(2,1)S(1)}, s32[]{:S(2)}) async-start(bf16[31,16,64]{2,1,0:T(8,128)(2,1)} %param.17), calls=%async_computation.3 | async-start | bytes 32768 | tf_op jit(solution)/shard_map/slice | solution.py:167
  46.7 2.8 %slice-start.4 = ((bf16[31,16,64]{2,1,0:T(8,128)(2,1)}), bf16[8,16,64]{2,1,0:T(8,128)(2,1)S(1)}, s32[]{:S(2)}) async-start(bf16[31,16,64]{2,1,0:T(8,128)(2,1)} %param.17), calls=%async_computation.4 | async-start | bytes 65536 | tf_op jit(solution)/shard_map/slice | solution.py:167
  46.7 2.9 %copy-start.14 = (s32[12,4]{0,1:T(4,128)S(1)}, s32[12,4]{0,1:T(4,128)}, u32[]{:S(2)}) copy-start(s32[12,4]{0,1:T(4,128)} %param.21) | copy-start | bytes 580
  47.9 15.8 %copy-start.10 = (bf16[12,16,64]{2,1,0:T(8,128)(2,1)S(1)}, bf16[12,16,64]{2,1,0:T(8,128)(2,1)}, u32[]{:S(2)}) copy-start(bf16[12,16,64]{2,1,0:T(8,128)(2,1)} %param.18) | copy-start | bytes 73732
  47.9 19.5 %copy-start.15 = (s32[16,8]{0,1:T(8,128)S(1)}, s32[16,8]{0,1:T(8,128)}, u32[]{:S(2)}) copy-start(s32[16,8]{0,1:T(8,128)} %param.19) | copy-start | bytes 1540
  48.1 43.6 %copy-start.2 = (bf16[31,16,64]{2,1,0:T(8,128)(2,1)S(1)}, bf16[31,16,64]{2,1,0:T(8,128)(2,1)}, u32[]{:S(2)}) copy-start(bf16[31,16,64]{2,1,0:T(8,128)(2,1)} %param.17) | copy-start | bytes 190468
  65.6 48.2 %copy-start.37 = (f32[2]{0:T(128)S(1)}, f32[2]{0:T(128)}, u32[]{:S(2)}) copy-start(f32[2]{0:T(128)} %get-tuple-element.31) | copy-start | bytes 28
  66.8 47.5 %copy-start.36 = (f32[2]{0:T(128)S(1)}, f32[2]{0:T(128)}, u32[]{:S(2)}) copy-start(f32[2]{0:T(128)} %get-tuple-element.30) | copy-start | bytes 28
  68.1 10.1 %collective-permute-start.14 = (bf16[1,3072]{1,0:T(2,128)(2,1)}, bf16[1,3072]{1,0:T(2,128)(2,1)S(1)}, u32[]{:S(2)}, u32[]{:S(2)}) collective-permute-start(bf16[1,3072]{1,0:T(2,128)(2,1)} %constant_dynamic-update-slice_fusion.10), channel_id=1, source_target_pairs={{0,2},{1,3},{2,4},{3,5},{4,6},{5,7},{6,8},{7,9},{8,10},{9,11},{10,... | collective-permute-start | bytes 18440 | tf_op jit(solution)/shard_map/ppermute | solution.py:103
  71.5 8.7 %collective-permute-start.15 = (bf16[1,3072]{1,0:T(2,128)(2,1)}, bf16[1,3072]{1,0:T(2,128)(2,1)S(1)}, u32[]{:S(2)}, u32[]{:S(2)}) collective-permute-start(bf16[1,3072]{1,0:T(2,128)(2,1)} %constant_dynamic-update-slice_fusion.10), channel_id=1, source_target_pairs={{2,0},{3,1},{4,2},{5,3},{6,4},{7,5},{8,6},{9,7},{10,8},{11,9},{12,... | collective-permute-start | bytes 18440 | tf_op jit(solution)/shard_map/ppermute | solution.py:103
  75.5 7.1 %collective-permute-start.16 = (bf16[1,3072]{1,0:T(2,128)(2,1)}, bf16[1,3072]{1,0:T(2,128)(2,1)S(1)}, u32[]{:S(2)}, u32[]{:S(2)}) collective-permute-start(bf16[1,3072]{1,0:T(2,128)(2,1)} %constant_dynamic-update-slice_fusion.10), channel_id=1, source_target_pairs={{3,0},{4,1},{5,2},{6,3},{7,4},{8,5},{9,6},{10,7},{11,8},{12,9},{13... | collective-permute-start | bytes 18440 | tf_op jit(solution)/shard_map/ppermute | solution.py:103
  78.2 19.8 %collective-permute-start.11 = (bf16[2,3072]{1,0:T(2,128)(2,1)}, bf16[2,3072]{1,0:T(2,128)(2,1)S(1)}, u32[]{:S(2)}, u32[]{:S(2)}) collective-permute-start(bf16[2,3072]{1,0:T(2,128)(2,1)} %constant_dynamic-update-slice_fusion.8), channel_id=1, source_target_pairs={{2,0},{3,1},{4,2},{5,3},{6,4},{7,5},{8,6},{9,7},{10,8},{11,9},{12,... | collective-permute-start | bytes 36872 | tf_op jit(solution)/shard_map/ppermute | solution.py:103
  80.1 21.9 %collective-permute-start.10 = (bf16[2,3072]{1,0:T(2,128)(2,1)}, bf16[2,3072]{1,0:T(2,128)(2,1)S(1)}, u32[]{:S(2)}, u32[]{:S(2)}) collective-permute-start(bf16[2,3072]{1,0:T(2,128)(2,1)} %constant_dynamic-update-slice_fusion.8), channel_id=1, source_target_pairs={{1,0},{2,1},{3,2},{4,3},{5,4},{6,5},{7,6},{8,7},{9,8},{10,9},{11,1... | collective-permute-start | bytes 36872 | tf_op jit(solution)/shard_map/ppermute | solution.py:103
  82.6 21.6 %collective-permute-start.9 = (bf16[2,3072]{1,0:T(2,128)(2,1)}, bf16[2,3072]{1,0:T(2,128)(2,1)S(1)}, u32[]{:S(2)}, u32[]{:S(2)}) collective-permute-start(bf16[2,3072]{1,0:T(2,128)(2,1)} %constant_dynamic-update-slice_fusion.8), channel_id=1, source_target_pairs={{0,1},{1,2},{2,3},{3,4},{4,5},{5,6},{6,7},{7,8},{8,9},{9,10},{10,1... | collective-permute-start | bytes 36872 | tf_op jit(solution)/shard_map/ppermute | solution.py:103
  87.2 27.5 %copy-start.16 = (f32[2]{0:T(128)S(1)}, f32[2]{0:T(128)}, u32[]{:S(2)}) copy-start(f32[2]{0:T(128)} %get-tuple-element.34) | copy-start | bytes 28
  90.0 25.0 %copy-start.35 = (f32[2]{0:T(128)S(1)}, f32[2]{0:T(128)}, u32[]{:S(2)}) copy-start(f32[2]{0:T(128)} %get-tuple-element.29) | copy-start | bytes 28
  98.0 10.7 %collective-permute-start.8 = (bf16[2,3072]{1,0:T(2,128)(2,1)}, bf16[2,3072]{1,0:T(2,128)(2,1)S(1)}, u32[]{:S(2)}, u32[]{:S(2)}) collective-permute-start(bf16[2,3072]{1,0:T(2,128)(2,1)} %constant_dynamic-update-slice_fusion.8), channel_id=1, source_target_pairs={{0,2},{1,3},{2,4},{3,5},{4,6},{5,7},{6,8},{7,9},{8,10},{9,11},{10,... | collective-permute-start | bytes 36872 | tf_op jit(solution)/shard_map/ppermute | solution.py:103
  102.0 14.3 %collective-permute-start.7 = (bf16[4,3072]{1,0:T(4,128)(2,1)S(1)}, bf16[4,3072]{1,0:T(4,128)(2,1)S(1)}, u32[]{:S(2)}, u32[]{:S(2)}) collective-permute-start(bf16[4,3072]{1,0:T(4,128)(2,1)S(1)} %constant_dynamic-update-slice_fusion.6), channel_id=1, source_target_pairs={{1,0},{2,1},{3,2},{4,3},{5,4},{6,5},{7,6},{8,7},{9,8},{10,9},{11,1... | collective-permute-start | bytes 73736 | tf_op jit(solution)/shard_map/ppermute | solution.py:103
  104.2 16.6 %collective-permute-start.6 = (bf16[4,3072]{1,0:T(4,128)(2,1)S(1)}, bf16[4,3072]{1,0:T(4,128)(2,1)S(1)}, u32[]{:S(2)}, u32[]{:S(2)}) collective-permute-start(bf16[4,3072]{1,0:T(4,128)(2,1)S(1)} %constant_dynamic-update-slice_fusion.6), channel_id=1, source_target_pairs={{0,1},{1,2},{2,3},{3,4},{4,5},{5,6},{6,7},{7,8},{8,9},{9,10},{10,1... | collective-permute-start | bytes 73736 | tf_op jit(solution)/shard_map/ppermute | solution.py:103
  108.7 23.4 %collective-permute-start.5 = (bf16[8,3072]{1,0:T(8,128)(2,1)S(1)}, bf16[8,3072]{1,0:T(8,128)(2,1)S(1)}, u32[]{:S(2)}, u32[]{:S(2)}) collective-permute-start(bf16[8,3072]{1,0:T(8,128)(2,1)S(1)} %constant_dynamic-update-slice_fusion.4), channel_id=1, source_target_pairs={{1,0},{2,1},{3,2},{4,3},{5,4},{6,5},{7,6},{8,7},{9,8},{10,9},{11,1... | collective-permute-start | bytes 147464 | tf_op jit(solution)/shard_map/ppermute | solution.py:103
  111.2 14.3 %copy-start.34 = (f32[4]{0:T(128)S(1)}, f32[4]{0:T(128)}, u32[]{:S(2)}) copy-start(f32[4]{0:T(128)} %get-tuple-element.25) | copy-start | bytes 52
  111.7 14.8 %copy-start.33 = (f32[4]{0:T(128)S(1)}, f32[4]{0:T(128)}, u32[]{:S(2)}) copy-start(f32[4]{0:T(128)} %get-tuple-element.24) | copy-start | bytes 52
  113.8 14.0 %copy-start.32 = (f32[4]{0:T(128)S(1)}, f32[4]{0:T(128)}, u32[]{:S(2)}) copy-start(f32[4]{0:T(128)} %get-tuple-element.28) | copy-start | bytes 52
  114.2 14.9 %copy-start.31 = (f32[4]{0:T(128)S(1)}, f32[4]{0:T(128)}, u32[]{:S(2)}) copy-start(f32[4]{0:T(128)} %get-tuple-element.26) | copy-start | bytes 52
  115.0 14.5 %copy-start.30 = (f32[4]{0:T(128)S(1)}, f32[4]{0:T(128)}, u32[]{:S(2)}) copy-start(f32[4]{0:T(128)} %get-tuple-element.27) | copy-start | bytes 52
  115.5 10.0 %copy-start.12 = (f32[16]{0:T(128)S(1)}, f32[16]{0:T(128)}, u32[]{:S(2)}) copy-start(f32[16]{0:T(128)} %copy-done.11) | copy-start | bytes 196
  115.5 14.5 %copy-start.29 = (f32[4]{0:T(128)S(1)}, f32[4]{0:T(128)}, u32[]{:S(2)}) copy-start(f32[4]{0:T(128)} %get-tuple-element.23) | copy-start | bytes 52
  116.3 20.6 %collective-permute-start.4 = (bf16[8,3072]{1,0:T(8,128)(2,1)S(1)}, bf16[8,3072]{1,0:T(8,128)(2,1)S(1)}, u32[]{:S(2)}, u32[]{:S(2)}) collective-permute-start(bf16[8,3072]{1,0:T(8,128)(2,1)S(1)} %constant_dynamic-update-slice_fusion.4), channel_id=1, source_target_pairs={{0,1},{1,2},{2,3},{3,4},{4,5},{5,6},{6,7},{7,8},{8,9},{9,10},{10,1... | collective-permute-start | bytes 147464 | tf_op jit(solution)/shard_map/ppermute | solution.py:103
  120.8 59.2 %collective-permute-start.1 = (bf16[48,4096]{1,0:T(8,128)(2,1)}, bf16[48,4096]{1,0:T(8,128)(2,1)}, u32[]{:S(2)}, u32[]{:S(2)}) collective-permute-start(bf16[48,4096]{1,0:T(8,128)(2,1)} %get-tuple-element.93), channel_id=1, source_target_pairs={{1,0},{2,1},{3,2},{4,3},{5,4},{6,5},{7,6},{8,7},{9,8},{10,9},{11,1... | collective-permute-start | bytes 1179656 | tf_op jit(solution)/shard_map/ppermute | solution.py:93
  131.2 9.9 %copy-start.28 = (f32[8]{0:T(128)S(1)}, f32[8]{0:T(128)}, u32[]{:S(2)}) copy-start(f32[8]{0:T(128)} %get-tuple-element.21) | copy-start | bytes 100
  132.1 47.9 %collective-permute-start = (bf16[48,4096]{1,0:T(8,128)(2,1)}, bf16[48,4096]{1,0:T(8,128)(2,1)}, u32[]{:S(2)}, u32[]{:S(2)}) collective-permute-start(bf16[48,4096]{1,0:T(8,128)(2,1)} %get-tuple-element.92), channel_id=1, source_target_pairs={{0,1},{1,2},{2,3},{3,4},{4,5},{5,6},{6,7},{7,8},{8,9},{9,10},{10,1... | collective-permute-start | bytes 1179656 | tf_op jit(solution)/shard_map/ppermute | solution.py:91
  136.9 5.4 %copy-start.27 = (f32[8]{0:T(128)S(1)}, f32[8]{0:T(128)}, u32[]{:S(2)}) copy-start(f32[8]{0:T(128)} %get-tuple-element.19) | copy-start | bytes 100
  137.2 7.3 %copy-start.26 = (f32[8]{0:T(128)S(1)}, f32[8]{0:T(128)}, u32[]{:S(2)}) copy-start(f32[8]{0:T(128)} %get-tuple-element.18) | copy-start | bytes 100
  137.6 8.9 %copy-start.25 = (f32[8]{0:T(128)S(1)}, f32[8]{0:T(128)}, u32[]{:S(2)}) copy-start(f32[8]{0:T(128)} %get-tuple-element.22) | copy-start | bytes 100
  140.0 8.6 %copy-start.24 = (f32[8]{0:T(128)S(1)}, f32[8]{0:T(128)}, u32[]{:S(2)}) copy-start(f32[8]{0:T(128)} %get-tuple-element.20) | copy-start | bytes 100
  141.2 9.0 %copy-start.23 = (f32[8]{0:T(128)S(1)}, f32[8]{0:T(128)}, u32[]{:S(2)}) copy-start(f32[8]{0:T(128)} %get-tuple-element.17) | copy-start | bytes 100
  142.3 6.3 %copy-start.7 = (bf16[8,64,32]{2,1,0:T(8,128)(2,1)S(1)}, bf16[8,64,32]{2,1,0:T(8,128)(2,1)}, u32[]{:S(2)}) copy-start(bf16[8,64,32]{2,1,0:T(8,128)(2,1)} %slice.550) | copy-start | bytes 98308
  154.6 5.7 %copy-start.6 = (bf16[16,2048]{1,0:T(8,128)(2,1)S(1)}, bf16[16,2048]{1,0:T(8,128)(2,1)}, u32[]{:S(2)}) copy-start(bf16[16,2048]{1,0:T(8,128)(2,1)} %get-tuple-element.97) | copy-start | bytes 196612
  154.6 9.2 %copy-start.13 = (f32[16]{0:T(128)S(1)}, f32[16]{0:T(128)}, u32[]{:S(2)}) copy-start(f32[16]{0:T(128)} %copy-done.11) | copy-start | bytes 196
  154.8 9.3 %copy-start.22 = (f32[16]{0:T(128)S(1)}, f32[16]{0:T(128)}, u32[]{:S(2)}) copy-start(f32[16]{0:T(128)} %get-tuple-element.56) | copy-start | bytes 196
  160.3 6.2 %copy-start.21 = (f32[16]{0:T(128)S(1)}, f32[16]{0:T(128)}, u32[]{:S(2)}) copy-start(f32[16]{0:T(128)} %get-tuple-element.52) | copy-start | bytes 196
  163.8 5.1 %copy-start.20 = (f32[16]{0:T(128)S(1)}, f32[16]{0:T(128)}, u32[]{:S(2)}) copy-start(f32[16]{0:T(128)} %get-tuple-element.53) | copy-start | bytes 196
  164.1 7.2 %copy-start.19 = (f32[16]{0:T(128)S(1)}, f32[16]{0:T(128)}, u32[]{:S(2)}) copy-start(f32[16]{0:T(128)} %get-tuple-element.54) | copy-start | bytes 196
  166.5 7.3 %copy-start.18 = (f32[16]{0:T(128)S(1)}, f32[16]{0:T(128)}, u32[]{:S(2)}) copy-start(f32[16]{0:T(128)} %get-tuple-element.55) | copy-start | bytes 196
  168.9 7.3 %copy-start.4 = (bf16[16,64,32]{2,1,0:T(8,128)(2,1)S(1)}, bf16[16,64,32]{2,1,0:T(8,128)(2,1)}, u32[]{:S(2)}) copy-start(bf16[16,64,32]{2,1,0:T(8,128)(2,1)} %slice.533) | copy-start | bytes 196612
  168.9 7.3 %copy-start.17 = (f32[16]{0:T(128)S(1)}, f32[16]{0:T(128)}, u32[]{:S(2)}) copy-start(f32[16]{0:T(128)} %get-tuple-element.51) | copy-start | bytes 196
  171.3 7.2 %copy-start.8 = (bf16[8,64,32]{1,2,0:T(8,128)(2,1)S(1)}, bf16[8,64,32]{1,2,0:T(8,128)(2,1)}, u32[]{:S(2)}) copy-start(bf16[8,64,32]{1,2,0:T(8,128)(2,1)} %fusion.109) | copy-start | bytes 98308

commit v2 on v1

v2 whole, which is shorter than its diff:
```python
import functools

import jax
import jax.numpy as jnp
from jax import lax
from jax.experimental import pallas as pl
from jax.experimental.pallas import tpu as pltpu
from jax.sharding import PartitionSpec as P

REACH = 8
CPL_REACH = 4

LOG2E = 1.4426950408889634


def split3(x):
    a = x.astype(jnp.bfloat16); r = x - a.astype(jnp.float32)
    b = r.astype(jnp.bfloat16); r = r - b.astype(jnp.float32)
    return a, b, r.astype(jnp.bfloat16)


def augment(points, inv):
    s = (points.astype(jnp.float32) * inv).astype(jnp.bfloat16)
    w = s.astype(jnp.float32)
    t1, t2, t3 = split3(w * LOG2E)
    n = (-0.5 * LOG2E) * jnp.sum(w * w, axis=-2, keepdims=True)
    n1, n2, n3 = (x.astype(jnp.float32) for x in split3(n))
    row = lax.broadcasted_iota(jnp.int32, w.shape, w.ndim - 2)
    nr = jnp.where(row % 3 == 0, n1, jnp.where(row % 3 == 1, n2, n3))
    src_n = jnp.where(row < 3, nr, jnp.where(row < 6, 1.0, 0.0)).astype(jnp.bfloat16)
    tgt_n = jnp.where(row < 3, 1.0, jnp.where(row < 6, nr, 0.0)).astype(jnp.bfloat16)
    return (jnp.concatenate([s, s, s, src_n], axis=-2), jnp.concatenate([t1, t2, t3, tgt_n], axis=-2))


NN = (((1,), (0,)), ((), ()))
NT = (((1,), (1,)), ((), ()))


def mul(a, b, dims=NN):
    return lax.dot_general(a, b, dims, preferred_element_type=jnp.float32)


def first_box(leaf_dev, height):
    return 2 * leaf_dev - 2 * (leaf_dev >> height)


def upward_kernel(basis_ref, vectors_ref, transfer_ref, skeleton_ref, own, head, tail, top):
    leaf_dev, _, leaf = basis_ref.shape
    probes = vectors_ref.shape[0]
    levels = leaf_dev.bit_length()
    own[:, probes:, :] = skeleton_ref[...]
    coefs = []
    for t in range(leaf_dev):
        c = mul(vectors_ref[:, t * leaf : (t + 1) * leaf], basis_ref[t], NT)
        coefs.append(c.astype(jnp.bfloat16))
        own[t, 0:probes, :] = coefs[-1]
    for height in range(levels - 1):
        row = first_box(leaf_dev, height)
        above = first_box(leaf_dev, height + 1)
        terms = [mul(c, transfer_ref[row + b]) for b, c in enumerate(coefs)]
        coefs = [(terms[2 * b] + terms[2 * b + 1]).astype(jnp.bfloat16) for b in range(len(terms) // 2)]
        for b, c in enumerate(coefs):
            own[above + b, 0:probes, :] = c
    near_rows = 0
    for height in range(levels):
        boxes = leaf_dev >> height
        row = first_box(leaf_dev, height)
        if boxes >= CPL_REACH:
            head[near_rows : near_rows + CPL_REACH] = own[row : row + CPL_REACH]
            tail[near_rows : near_rows + CPL_REACH] = own[row + boxes - CPL_REACH : row + boxes]
            near_rows += CPL_REACH
        else:
            top[...] = own[row:]
            break


def vmem(count):
    return [pl.BlockSpec(memory_space=pltpu.VMEM)] * count


def upward(leaf_basis, vectors, transfer, skeleton):
    leaf_dev, rank, _ = leaf_basis.shape
    rows = vectors.shape[0] + skeleton.shape[1]
    edge = sum(CPL_REACH for h in range(leaf_dev.bit_length()) if leaf_dev >> h >= CPL_REACH)
    high = sum(leaf_dev >> h for h in range(leaf_dev.bit_length()) if leaf_dev >> h < CPL_REACH)
    shapes = [(n, rows, rank) for n in (skeleton.shape[0], edge, edge, high)]
    return pl.pallas_call(
        upward_kernel,
        in_specs=vmem(4),
        out_specs=vmem(4),
        out_shape=[jax.ShapeDtypeStruct(s, jnp.bfloat16) for s in shapes],
        cost_estimate=pl.CostEstimate(flops=4 * 10**9, bytes_accessed=4 << 20, transcendentals=0),
        compiler_params=pltpu.CompilerParams(vmem_limit_bytes=24 << 20),
    )(leaf_basis, vectors, transfer, skeleton)


def near_kernel(off_ref, inv_ref, left_ref, points_ref, vectors_ref, right_ref, out_ref, src, tgt, vec):
    leaf_dev, near = off_ref.shape
    dims = points_ref.shape[0]
    rows = left_ref.shape[0]
    leaf = points_ref.shape[1] // leaf_dev
    inv = inv_ref[...]

    def part(b):
        return pl.ds(pl.multiple_of(b * leaf, leaf), leaf)

    def side(ref, at):
        def step(b, _):
            s, _t = augment(ref[0:dims, part(b)], inv)
            src[part(at + b), :] = s.T
            vec[:, part(at + b)] = ref[dims:rows, part(b)]
            return 0

        lax.fori_loop(0, REACH, step, 0)

    def middle(b, _):
        s, t = augment(points_ref[:, part(b)], inv)
        src[part(REACH + b), :] = s.T
        tgt[:, part(b)] = t
        vec[:, part(REACH + b)] = vectors_ref[:, part(b)]
        return 0

    side(left_ref, 0)
    lax.fori_loop(0, leaf_dev, middle, 0)
    side(right_ref, REACH + leaf_dev)

    def one(t, _):
        acc = None
        target = tgt[:, part(t)]
        for m in range(near):
            col = part(t + REACH + off_ref[t, m])
            k = jnp.exp2(mul(src[col, :], target)).astype(jnp.bfloat16)
            d = mul(vec[:, col], k)
            acc = d if acc is None else acc + d
        out_ref[:, part(t)] = acc
        return 0

    lax.fori_loop(0, leaf_dev, one, 0)


def near_product(offsets, inverse, left, points, vectors, right):
    dims, count = points.shape
    probes = vectors.shape[0]
    width = count + left.shape[1] + right.shape[1]
    depth = 4 * dims
    return pl.pallas_call(
        near_kernel,
        in_specs=[pl.BlockSpec(memory_space=pltpu.SMEM)] + vmem(5),
        out_specs=pl.BlockSpec(memory_space=pltpu.VMEM),
        out_shape=jax.ShapeDtypeStruct((probes, count), jnp.float32),
        scratch_shapes=[
            pltpu.VMEM((width, depth), jnp.bfloat16),
            pltpu.VMEM((depth, count), jnp.bfloat16),
            pltpu.VMEM((probes, width), jnp.bfloat16),
        ],
        cost_estimate=pl.CostEstimate(flops=40 * 10**9, bytes_accessed=4 << 20, transcendentals=33 << 20),
        compiler_params=pltpu.CompilerParams(vmem_limit_bytes=32 << 20),
    )(offsets, inverse, left, points, vectors, right)


def far_kernel(
    seg_count, place_ref, local_ref, upper_ref, inv_ref, basis_ref, transfer_ref, up_transfer_ref, up_skeleton_ref,
    own_ref, left_ref, right_ref, top_ref, near_ref, out_ref, win, high, src, tgt,
):
    leaf_dev, rank, leaf = basis_ref.shape
    probes = near_ref.shape[0]
    levels = leaf_dev.bit_length()
    cross = seg_count.bit_length() - 3
    pad = CPL_REACH
    place = place_ref[0]
    high[...] = jnp.zeros_like(high)
    at = 0
    edge = 0
    store = 0
    offset = 0
    starts = []
    for height in range(levels):
        boxes = leaf_dev >> height
        row = first_box(leaf_dev, height)
        starts.append(at)
        if boxes >= pad:
            win[at : at + pad] = left_ref[edge : edge + pad]
            win[at + pad : at + pad + boxes] = own_ref[row : row + boxes]
            win[at + pad + boxes : at + 2 * pad + boxes] = right_ref[edge : edge + pad]
            edge += pad
        else:
            for g in range(seg_count):
                spot = store + pad + g * boxes
                high[spot : spot + boxes] = top_ref[g, offset : offset + boxes]
            win[at : at + 2 * pad + boxes] = high[pl.ds(store + place * boxes, 2 * pad + boxes)]
            offset += boxes
            if height < levels - 1:
                store += 2 * pad + boxes * seg_count
        at += 2 * pad + boxes
    for above in range(1, cross + 1):
        boxes = seg_count >> above
        row = 2 * seg_count - 4 * boxes
        skel_row = seg_count - 2 * boxes
        below = store + pad
        store += 2 * pad + 2 * boxes
        for b in range(boxes):
            c = mul(high[below + 2 * b, 0:probes, :], up_transfer_ref[row + 2 * b]) + mul(
                high[below + 2 * b + 1, 0:probes, :], up_transfer_ref[row + 2 * b + 1]
            )
            high[store + pad + b, 0:probes, :] = c.astype(jnp.bfloat16)
            high[store + pad + b, probes:, :] = up_skeleton_ref[skel_row + b]
        starts.append(at)
        win[at : at + 2 * pad + 1] = high[pl.ds(store + place // (1 << above), 2 * pad + 1)]
        at += 2 * pad + 1
    inv = inv_ref[...]
    for r in range(at):
        s, t = augment(win[r, probes:, :], inv)
        src[r * rank : (r + 1) * rank, :] = s.T
        tgt[r] = t

    def coupled(base, list_ref, row):
        picks = [base + list_ref[row, m] for m in range(list_ref.shape[1])]
        stacked = jnp.concatenate([src[pl.ds(pl.multiple_of(p * rank, rank), rank), :] for p in picks], axis=0)
        k = jnp.exp2(mul(stacked, tgt[base])).astype(jnp.bfloat16)
        total = None
        for m, p in enumerate(picks):
            d = mul(win[p, 0:probes, :], k[m * rank : (m + 1) * rank])
            total = d if total is None else total + d
        return total

    field = None
    for above in range(cross, 0, -1):
        boxes = seg_count >> above
        position = place // (1 << above)
        own = coupled(starts[levels - 1 + above] + pad, upper_ref, seg_count - 2 * boxes + position)
        if field is not None:
            own = own + mul(field, up_transfer_ref[2 * seg_count - 2 * boxes + position], NT)
        field = own.astype(jnp.bfloat16)
    spread = mul(field, up_transfer_ref[place], NT)
    fields = None
    for height in range(levels - 1, -1, -1):
        boxes = leaf_dev >> height
        row = first_box(leaf_dev, height)
        now = []
        for b in range(boxes):
            own = coupled(starts[height] + pad + b, local_ref, row + b)
            if fields is None:
                own = own + spread
            else:
                own = own + mul(fields[b // 2], transfer_ref[row + b], NT)
            now.append(own.astype(jnp.bfloat16))
        fields = now
    for t in range(leaf_dev):
        cols = slice(t * leaf, (t + 1) * leaf)
        out_ref[:, cols] = near_ref[:, cols] + mul(fields[t], basis_ref[t])


def far_sum(
    seg_count, place, local_coupling, upper_coupling, inverse, leaf_basis, local_transfer, upper_transfer,
    upper_skeleton, own, left, right, top, near_part,
):
    leaf_dev, rank, _ = leaf_basis.shape
    rows = own.shape[1]
    dims = upper_skeleton.shape[1]
    pad = 2 * CPL_REACH
    counts = [leaf_dev >> h for h in range(leaf_dev.bit_length())]
    uppers = [seg_count >> a for a in range(1, seg_count.bit_length() - 2)]
    window = sum(n + pad for n in counts) + len(uppers) * (pad + 1)
    high = sum(n * seg_count + pad for n in counts if n < CPL_REACH) + sum(n + pad for n in uppers)
    return pl.pallas_call(
        functools.partial(far_kernel, seg_count),
        in_specs=[pl.BlockSpec(memory_space=pltpu.SMEM)] * 3 + vmem(10),
        out_specs=pl.BlockSpec(memory_space=pltpu.VMEM),
        out_shape=jax.ShapeDtypeStruct(near_part.shape, jnp.float32),
        scratch_shapes=[
            pltpu.VMEM((window, rows, rank), jnp.bfloat16),
            pltpu.VMEM((high, rows, rank), jnp.bfloat16),
            pltpu.VMEM((window * rank, 4 * dims), jnp.bfloat16),
            pltpu.VMEM((window, 4 * dims, rank), jnp.bfloat16),
        ],
        cost_estimate=pl.CostEstimate(flops=10**10, bytes_accessed=6 << 20, transcendentals=1 << 20),
        compiler_params=pltpu.CompilerParams(vmem_limit_bytes=40 << 20),
    )(
        place, local_coupling, upper_coupling, inverse, leaf_basis, local_transfer, upper_transfer, upper_skeleton,
        own, left, right, top, near_part,
    )


def body(
    points,
    vectors,
    lengthscale,
    leaf_basis,
    local_transfer,
    upper_transfer,
    local_skeleton,
    upper_skeleton,
    near_offsets,
    local_coupling,
    upper_coupling,
):
    inverse = (1.0 / lengthscale)[:, None]
    leaf = leaf_basis.shape[2]
    count = points.shape[1]
    seg_count = lax.axis_size("seg")
    place = lax.axis_index("seg").astype(jnp.int32)[None]
    ahead = [(i, i + 1) for i in range(seg_count - 1)]
    back = [(i + 1, i) for i in range(seg_count - 1)]
    reach = REACH * leaf
    first = jnp.concatenate([points[:, :reach], vectors[:, :reach]], axis=0)
    last = jnp.concatenate([points[:, count - reach :], vectors[:, count - reach :]], axis=0)
    left = lax.ppermute(last, "seg", ahead)
    right = lax.ppermute(first, "seg", back)
    own, head, tail, top = upward(leaf_basis, vectors, local_transfer, local_skeleton)
    far_left = lax.ppermute(tail, "seg", ahead)
    far_right = lax.ppermute(head, "seg", back)
    far_top = lax.all_gather(top, "seg", axis=0, tiled=False)
    near_part = near_product(near_offsets, inverse, left, points, vectors, right)
    return far_sum(
        seg_count, place, local_coupling, upper_coupling, inverse, leaf_basis, local_transfer, upper_transfer,
        upper_skeleton, own, far_left, far_right, far_top, near_part,
    )


def solution(mesh):
    in_specs = (
        P(None, ("groups", "seg")),
        P(None, ("groups", "seg")),
        P("groups"),
        P(("groups", "seg"), None, None),
        P(("groups", "seg"), None, None),
        P("groups", None, None),
        P(("groups", "seg"), None, None),
        P("groups", None, None),
        P(("groups", "seg"), None),
        P(("groups", "seg"), None),
        P("groups", None),
    )
    out_specs = P(None, ("groups", "seg"))
    return jax.shard_map(body, mesh=mesh, in_specs=in_specs, out_specs=out_specs, check_vma=False)
```

time: 230 us -> 95.4 us (0.41)
  the two profiles are of different devices: /device:TPU:5 before, /device:TPU:1 now
where the time goes in v2:
time: 95.4 us; the launch traced here: 95 us
  Pallas kernels  52.6 us (55%)
  blocking collectives  23.8 us (25%)
  starting transfers between devices  12.1 us (13%)
  local copies, waits for them, and re-layouts  4.77 us (5%)
  other arithmetic  1.55 us (2%)
    pallas_call x1, Pallas kernels, near_product(): pl.pallas_call(near_kernel, in_specs=[pl.BlockSpec(memory_space=pltpu.SME...  44.8 us
    all_gather x1, blocking collectives, body(): far_top = lax.all_gather(top, 'seg', axis=0, tiled=False)  23.8 us
    pallas_call x1, Pallas kernels, far_sum(): pl.pallas_call(functools.partial(far_kernel, seg_count), in_specs=[pl.Blo...  6.77 us
    ppermute x1, starting transfers between devices, body(): left = lax.ppermute(last, 'seg', ahead)  4.66 us
    ppermute x1, starting transfers between devices, body(): far_left = lax.ppermute(tail, 'seg', ahead)  3.63 us
    unnamed x29, local copies, waits for them, and re-layouts  3.61 us
    ppermute x1, starting transfers between devices, body(): far_right = lax.ppermute(head, 'seg', back)  1.92 us
  transfers between devices with their start and end apart: 4, of which 0 were waited for; matrix products, arithmetic and copies ran while one was open for 1% of the time, Pallas kernels for 48%

profile of v2, /device:TPU:1, one launch (start us, length us, event | category | flops | bytes accessed | tf_op | source)
XLA Modules:
  0.0 95.0 jit_solution(5530248484413114271)
XLA Ops:
  0.0 0.0 copy-start
  0.0 1.0 %fusion.1 = (bf16[16,4096]{1,0:T(8,128)(2,1)S(1)}, bf16[16,4096]{1,0:T(8,128)(2,1)S(1)}) fusion(bf16[16,8192]{1,0:T(8,128)(2,1)} %points_ref.1), kind=kLoop, calls=%fused_computation.4 | loop fusion | bytes 524288 | tf_op jit(solution)/shard_map/slice | solution.py:305
  1.0 0.1 copy-done
  1.2 0.0 copy-start.5
  1.2 0.0 copy-start.2
  1.2 0.8 pad_maximum_fusion
  2.0 0.0 copy-start.3
  2.0 4.7 %collective-permute-start.2 = (bf16[48,4096]{1,0:T(8,128)(2,1)}, bf16[48,4096]{1,0:T(8,128)(2,1)S(1)}, u32[]{:S(2)}, u32[]{:S(2)}) collective-permute-start(bf16[48,4096]{1,0:T(8,128)(2,1)} %pad_maximum_fusion), channel_id=1, source_target_pairs={{0,1},{1,2},{2,3},{3,4},{4,5},{5,6},{6,7},{7,8},{8,9},{9,10},{10,1... | collective-permute-start | bytes 1179656 | tf_op jit(solution)/shard_map/ppermute | solution.py:307
  6.7 0.8 pad_maximum_fusion.1
  7.4 1.9 %collective-permute-start.3 = (bf16[48,4096]{1,0:T(8,128)(2,1)}, bf16[48,4096]{1,0:T(8,128)(2,1)S(1)}, u32[]{:S(2)}, u32[]{:S(2)}) collective-permute-start(bf16[48,4096]{1,0:T(8,128)(2,1)} %pad_maximum_fusion.1), channel_id=1, source_target_pairs={{1,0},{2,1},{3,2},{4,3},{5,4},{6,5},{7,6},{8,7},{9,8},{10,9},{11,1... | collective-permute-start | bytes 1179656 | tf_op jit(solution)/shard_map/ppermute | solution.py:308
  9.3 0.0 copy-done.5
  9.4 0.0 copy-done.2
  9.4 0.0 copy-done.3
  9.4 1.0 %shard_map.109 = (bf16[31,48,64]{2,1,0:T(8,128)(2,1)S(1)}, bf16[12,48,64]{2,1,0:T(8,128)(2,1)S(1)}, bf16[12,48,64]{2,1,0:T(8,128)(2,1)S(1)}, bf16[3,48,64]{2,1,0:T(8,128)(2,1)S(1)}) custom-call(bf16[16,64,512]{2,1,0:T(8,128)(2,1)S(1)} %copy-done.2, bf16[32,8192]{1,0:T(8,128)(2,1)S(1)} %copy-done, bf16[30,64,64]{2,1,0:T(8,128)(2,1)S(1)} %copy-done.3, ...), custom_call_target="tpu_custom_call" | custom-call | flops 4000000000 | bytes 4194304 | tf_op jit(solution)/shard_map/pallas_call | solution.py:87
  10.4 0.0 copy-start.7
  10.4 0.7 copy-done.7
  11.1 3.6 %collective-permute-start = (bf16[12,48,64]{2,1,0:T(8,128)(2,1)S(1)}, bf16[12,48,64]{2,1,0:T(8,128)(2,1)S(1)}, u32[]{:S(2)}, u32[]{:S(2)}) collective-permute-start(bf16[12,48,64]{2,1,0:T(8,128)(2,1)S(1)} %get-tuple-element.10), channel_id=1, source_target_pairs={{0,1},{1,2},{2,3},{3,4},{4,5},{5,6},{6,7},{7,8},{8,9},{9,10},{10,1... | collective-permute-start | bytes 221192 | tf_op jit(solution)/shard_map/ppermute | solution.py:310
  14.7 1.9 %collective-permute-start.1 = (bf16[12,48,64]{2,1,0:T(8,128)(2,1)S(1)}, bf16[12,48,64]{2,1,0:T(8,128)(2,1)S(1)}, u32[]{:S(2)}, u32[]{:S(2)}) collective-permute-start(bf16[12,48,64]{2,1,0:T(8,128)(2,1)S(1)} %get-tuple-element.11), channel_id=1, source_target_pairs={{1,0},{2,1},{3,2},{4,3},{5,4},{6,5},{7,6},{8,7},{9,8},{10,9},{11,1... | collective-permute-start | bytes 221192 | tf_op jit(solution)/shard_map/ppermute | solution.py:311
  16.7 0.0 copy-start.12
  16.7 0.6 copy-done.12
  17.3 0.0 copy-start.9
  17.3 0.1 copy.21.inv_ref
  17.4 0.6 copy-done.9
  18.0 0.0 copy-start.10
  18.0 0.1 copy.17.off_ref
  18.1 0.6 copy-done.10
  18.7 0.0 copy-start.11
  18.7 0.1 copy.20.upper_ref
  18.8 0.6 copy-done.11
  19.4 0.1 copy.19.local_ref
  19.5 0.0 copy-start.1
  19.5 23.8 %all-gather = bf16[48,48,64]{2,1,0:T(8,128)(2,1)S(1)} all-gather(bf16[3,48,64]{2,1,0:T(8,128)(2,1)S(1)} %get-tuple-element.12), channel_id=2, replica_groups=mesh['groups'=2,'seg'=16] {'seg'}, dimensions={0}, use_global_device_ids=true | all-gather | bytes 313344 | tf_op jit(solution)/shard_map/all_gather | solution.py:312
  43.3 0.0 copy-start.4
  43.3 0.0 copy-start.6
  43.3 0.0 copy-start.8
  43.3 0.0 collective-permute-done.2.left_ref
  43.3 0.0 collective-permute-done.3.right_ref
  43.3 0.0 copy-done.1
  43.3 44.8 %shard_map.110.near_ref = f32[32,8192]{1,0:T(8,128)S(1)} custom-call(s32[16,8]{1,0:T(8,128)S(1)} %copy.17.off_ref, f32[16,1]{1,0:T(8,128)S(1)} %copy.21.inv_ref, bf16[48,4096]{1,0:T(8,128)(2,1)S(1)} %collective-permute-done.2.left_ref, bf16[16,8192]{1,0:T(8,128)(2,1)S(1)} %copy-done.1, bf16[32,8192]{1,0:T(8,128)(2,1)S(1)} %copy-done, ...), custom_call_target="tpu_custom_call" | custom-call | flops 40000000000 | bytes 4194304 | tf_op jit(solution)/shard_map/pallas_call | solution.py:146
  88.2 0.0 collective-permute-done.left_ref
  88.2 0.0 collective-permute-done.1.right_ref
  88.2 0.0 copy-done.4
  88.2 0.0 copy-done.6
  88.2 0.0 copy-done.8
  88.2 6.8 %shard_map.111 = f32[32,8192]{1,0:T(8,128)} custom-call(s32[1]{0:T(128)} %bitcast.place_ref, s32[31,4]{1,0:T(8,128)S(1)} %copy.19.local_ref, s32[12,4]{1,0:T(8,128)S(1)} %copy.20.upper_ref, f32[16,1]{1,0:T(8,128)S(1)} %copy.21.inv_ref, bf16[16,64,512]{2,1,0:T(8,128)(2,1)S(1)} %copy-done.2, bf16[30,64,64]{2,1,0:T(8,128)(2,1)S(1)} %copy-done.3, ...), custom_call_target="tpu_custom_call" | custom-call | flops 10000000000 | bytes 6291456 | tf_op jit(solution)/shard_map/pallas_call | solution.py:265
  (2 shorter events, 0.0 us)
Async XLA Ops:
  0.0 1.2 %copy-start = (bf16[32,8192]{1,0:T(8,128)(2,1)S(1)}, bf16[32,8192]{1,0:T(8,128)(2,1)}, u32[]{:S(2)}) copy-start(bf16[32,8192]{1,0:T(8,128)(2,1)} %vectors_ref.3) | copy-start | bytes 1572868
  1.2 8.2 %copy-start.5 = (bf16[31,16,64]{2,1,0:T(8,128)(2,1)S(1)}, bf16[31,16,64]{2,1,0:T(8,128)(2,1)}, u32[]{:S(2)}) copy-start(bf16[31,16,64]{2,1,0:T(8,128)(2,1)} %skeleton_ref.1) | copy-start | bytes 190468
  1.2 8.2 %copy-start.2 = (bf16[16,64,512]{2,1,0:T(8,128)(2,1)S(1)}, bf16[16,64,512]{2,1,0:T(8,128)(2,1)}, u32[]{:S(2)}) copy-start(bf16[16,64,512]{2,1,0:T(8,128)(2,1)} %basis_ref.3) | copy-start | bytes 3145732
  2.0 7.4 %copy-start.3 = (bf16[30,64,64]{2,1,0:T(8,128)(2,1)S(1)}, bf16[30,64,64]{2,1,0:T(8,128)(2,1)}, u32[]{:S(2)}) copy-start(bf16[30,64,64]{2,1,0:T(8,128)(2,1)} %transfer_ref.3) | copy-start | bytes 737284
  2.0 41.3 %collective-permute-start.2 = (bf16[48,4096]{1,0:T(8,128)(2,1)}, bf16[48,4096]{1,0:T(8,128)(2,1)S(1)}, u32[]{:S(2)}, u32[]{:S(2)}) collective-permute-start(bf16[48,4096]{1,0:T(8,128)(2,1)} %pad_maximum_fusion), channel_id=1, source_target_pairs={{0,1},{1,2},{2,3},{3,4},{4,5},{5,6},{6,7},{7,8},{8,9},{9,10},{10,1... | collective-permute-start | bytes 1179656 | tf_op jit(solution)/shard_map/ppermute | solution.py:307
  7.4 35.9 %collective-permute-start.3 = (bf16[48,4096]{1,0:T(8,128)(2,1)}, bf16[48,4096]{1,0:T(8,128)(2,1)S(1)}, u32[]{:S(2)}, u32[]{:S(2)}) collective-permute-start(bf16[48,4096]{1,0:T(8,128)(2,1)} %pad_maximum_fusion.1), channel_id=1, source_target_pairs={{1,0},{2,1},{3,2},{4,3},{5,4},{6,5},{7,6},{8,7},{9,8},{10,9},{11,1... | collective-permute-start | bytes 1179656 | tf_op jit(solution)/shard_map/ppermute | solution.py:308
  10.4 0.7 copy-start.7
  11.1 77.1 %collective-permute-start = (bf16[12,48,64]{2,1,0:T(8,128)(2,1)S(1)}, bf16[12,48,64]{2,1,0:T(8,128)(2,1)S(1)}, u32[]{:S(2)}, u32[]{:S(2)}) collective-permute-start(bf16[12,48,64]{2,1,0:T(8,128)(2,1)S(1)} %get-tuple-element.10), channel_id=1, source_target_pairs={{0,1},{1,2},{2,3},{3,4},{4,5},{5,6},{6,7},{7,8},{8,9},{9,10},{10,1... | collective-permute-start | bytes 221192 | tf_op jit(solution)/shard_map/ppermute | solution.py:310
  14.7 73.5 %collective-permute-start.1 = (bf16[12,48,64]{2,1,0:T(8,128)(2,1)S(1)}, bf16[12,48,64]{2,1,0:T(8,128)(2,1)S(1)}, u32[]{:S(2)}, u32[]{:S(2)}) collective-permute-start(bf16[12,48,64]{2,1,0:T(8,128)(2,1)S(1)} %get-tuple-element.11), channel_id=1, source_target_pairs={{1,0},{2,1},{3,2},{4,3},{5,4},{6,5},{7,6},{8,7},{9,8},{10,9},{11,1... | collective-permute-start | bytes 221192 | tf_op jit(solution)/shard_map/ppermute | solution.py:311
  16.7 0.7 copy-start.12
  17.3 0.7 copy-start.9
  18.0 0.7 copy-start.10
  18.7 0.7 copy-start.11
  19.5 23.8 %copy-start.1 = (bf16[16,8192]{1,0:T(8,128)(2,1)S(1)}, bf16[16,8192]{1,0:T(8,128)(2,1)}, u32[]{:S(2)}) copy-start(bf16[16,8192]{1,0:T(8,128)(2,1)} %points_ref.1) | copy-start | bytes 786436
  43.3 44.9 %copy-start.4 = (bf16[24,64,64]{2,1,0:T(8,128)(2,1)S(1)}, bf16[24,64,64]{2,1,0:T(8,128)(2,1)}, u32[]{:S(2)}) copy-start(bf16[24,64,64]{2,1,0:T(8,128)(2,1)} %up_transfer_ref.1) | copy-start | bytes 589828
  43.3 44.9 %copy-start.6 = (bf16[12,16,64]{2,1,0:T(8,128)(2,1)S(1)}, bf16[12,16,64]{2,1,0:T(8,128)(2,1)}, u32[]{:S(2)}) copy-start(bf16[12,16,64]{2,1,0:T(8,128)(2,1)} %up_skeleton_ref.1) | copy-start | bytes 73732
  43.3 44.9 %copy-start.8 = (bf16[31,48,64]{2,1,0:T(8,128)(2,1)S(1)}, bf16[31,48,64]{2,1,0:T(8,128)(2,1)}, u32[]{:S(2)}) copy-start(bf16[31,48,64]{2,1,0:T(8,128)(2,1)} %copy-done.7) | copy-start | bytes 571396

commit v3 on v2

--- a/solution.py
+++ b/solution.py
@@ -44,7 +44,60 @@
     return 2 * leaf_dev - 2 * (leaf_dev >> height)
 
 
-def upward_kernel(basis_ref, vectors_ref, transfer_ref, skeleton_ref, own, head, tail, top):
+MESH = pl.DeviceIdType.MESH
+
+
+def upward_kernel(
+    seg_count, basis_ref, points_ref, vectors_ref, transfer_ref, skeleton_ref,
+    own, left_p, left_v, right_p, right_v, far_left, far_right, far_top,
+    head, tail, top, send, recv, top_send, top_recv,
+):
+    me = lax.axis_index("seg")
+    reach = left_p.shape[1]
+    count = points_ref.shape[1]
+    barrier = pltpu.get_barrier_semaphore()
+
+    def greet(d, _):
+        pl.semaphore_signal(barrier, inc=1, device_id={"seg": lax.rem(me + d, seg_count)}, device_id_type=MESH)
+        return 0
+
+    lax.fori_loop(1, seg_count, greet, 0)
+    pl.semaphore_wait(barrier, seg_count - 1)
+
+    def link(k, source, target, peer):
+        return pltpu.make_async_remote_copy(
+            src_ref=source, dst_ref=target, send_sem=send.at[k], recv_sem=recv.at[k],
+            device_id={"seg": peer}, device_id_type=MESH,
+        )
+
+    end = pl.ds(count - reach, reach)
+    ahead = lambda: [
+        link(0, points_ref.at[:, end], left_p, me + 1),
+        link(1, vectors_ref.at[:, end], left_v, me + 1),
+    ]
+    back = lambda: [
+        link(2, points_ref.at[:, pl.ds(0, reach)], right_p, me - 1),
+        link(3, vectors_ref.at[:, pl.ds(0, reach)], right_v, me - 1),
+    ]
+    far_ahead = lambda: [link(4, tail, far_left, me + 1)]
+    far_back = lambda: [link(5, head, far_right, me - 1)]
+
+    def spread(d):
+        return pltpu.make_async_remote_copy(
+            src_ref=top, dst_ref=far_top.at[me], send_sem=top_send.at[d], recv_sem=top_recv.at[d],
+            device_id={"seg": lax.rem(me + d, seg_count)}, device_id_type=MESH,
+        )
+
+    @pl.when(me < seg_count - 1)
+    def _():
+        for copy in ahead():
+            copy.start()
+
+    @pl.when(me > 0)
+    def _():
+        for copy in back():
+            copy.start()
+
     leaf_dev, _, leaf = basis_ref.shape
     probes = vectors_ref.shape[0]
     levels = leaf_dev.bit_length()
@@ -72,43 +125,102 @@
         else:
             top[...] = own[row:]
             break
+    far_top[me] = top[...]
+
+    def start(d, _):
+        spread(d).start()
+        return 0
+
+    lax.fori_loop(1, seg_count, start, 0)
+
+    @pl.when(me < seg_count - 1)
+    def _():
+        far_ahead()[0].start()
+
+    @pl.when(me > 0)
+    def _():
+        far_back()[0].start()
+
+    @pl.when(me < seg_count - 1)
+    def _():
+        for copy in ahead() + far_ahead():
+            copy.wait_send()
+        for copy in back() + far_back():
+            copy.wait_recv()
+
+    @pl.when(me > 0)
+    def _():
+        for copy in back() + far_back():
+            copy.wait_send()
+        for copy in ahead() + far_ahead():
+            copy.wait_recv()
+
+    @pl.when(me == 0)
+    def _():
+        for ref in (left_p, left_v, far_left):
+            ref[...] = jnp.zeros_like(ref)
+
+    @pl.when(me == seg_count - 1)
+    def _():
+        for ref in (right_p, right_v, far_right):
+            ref[...] = jnp.zeros_like(ref)
+
+    def finish(d, _):
+        spread(d).wait()
+        return 0
+
+    lax.fori_loop(1, seg_count, finish, 0)
 
 
 def vmem(count):
     return [pl.BlockSpec(memory_space=pltpu.VMEM)] * count
 
 
-def upward(leaf_basis, vectors, transfer, skeleton):
-    leaf_dev, rank, _ = leaf_basis.shape
-    rows = vectors.shape[0] + skeleton.shape[1]
+def upward(seg_count, leaf_basis, points, vectors, transfer, skeleton):
+    leaf_dev, rank, leaf = leaf_basis.shape
+    dims, probes = points.shape[0], vectors.shape[0]
+    rows = probes + dims
+    reach = REACH * leaf
     edge = sum(CPL_REACH for h in range(leaf_dev.bit_length()) if leaf_dev >> h >= CPL_REACH)
     high = sum(leaf_dev >> h for h in range(leaf_dev.bit_length()) if leaf_dev >> h < CPL_REACH)
-    shapes = [(n, rows, rank) for n in (skeleton.shape[0], edge, edge, high)]
+    shapes = [
+        (skeleton.shape[0], rows, rank), (dims, reach), (probes, reach), (dims, reach), (probes, reach),
+        (edge, rows, rank), (edge, rows, rank), (seg_count, high, rows, rank),
+    ]
     return pl.pallas_call(
-        upward_kernel,
-        in_specs=vmem(4),
-        out_specs=vmem(4),
+        functools.partial(upward_kernel, seg_count),
+        in_specs=vmem(5),
+        out_specs=vmem(8),
         out_shape=[jax.ShapeDtypeStruct(s, jnp.bfloat16) for s in shapes],
+        scratch_shapes=[
+            pltpu.VMEM((edge, rows, rank), jnp.bfloat16),
+            pltpu.VMEM((edge, rows, rank), jnp.bfloat16),
+            pltpu.VMEM((high, rows, rank), jnp.bfloat16),
+            pltpu.SemaphoreType.DMA((6,)),
+            pltpu.SemaphoreType.DMA((6,)),
+            pltpu.SemaphoreType.DMA((seg_count,)),
+            pltpu.SemaphoreType.DMA((seg_count,)),
+        ],
         cost_estimate=pl.CostEstimate(flops=4 * 10**9, bytes_accessed=4 << 20, transcendentals=0),
-        compiler_params=pltpu.CompilerParams(vmem_limit_bytes=24 << 20),
-    )(leaf_basis, vectors, transfer, skeleton)
-
-
-def near_kernel(off_ref, inv_ref, left_ref, points_ref, vectors_ref, right_ref, out_ref, src, tgt, vec):
+        compiler_params=pltpu.CompilerParams(vmem_limit_bytes=24 << 20, collective_id=0, has_side_effects=True),
+    )(leaf_basis, points, vectors, transfer, skeleton)
+
+
+def near_kernel(
+    off_ref, inv_ref, left_p, left_v, points_ref, vectors_ref, right_p, right_v, out_ref, src, tgt, vec
+):
     leaf_dev, near = off_ref.shape
-    dims = points_ref.shape[0]
-    rows = left_ref.shape[0]
     leaf = points_ref.shape[1] // leaf_dev
     inv = inv_ref[...]
 
     def part(b):
         return pl.ds(pl.multiple_of(b * leaf, leaf), leaf)
 
-    def side(ref, at):
+    def side(pts, vcs, at):
         def step(b, _):
-            s, _t = augment(ref[0:dims, part(b)], inv)
+            s, _t = augment(pts[:, part(b)], inv)
             src[part(at + b), :] = s.T
-            vec[:, part(at + b)] = ref[dims:rows, part(b)]
+            vec[:, part(at + b)] = vcs[:, part(b)]
             return 0
 
         lax.fori_loop(0, REACH, step, 0)
@@ -120,9 +232,9 @@
         vec[:, part(REACH + b)] = vectors_ref[:, part(b)]
         return 0
 
-    side(left_ref, 0)
+    side(left_p, left_v, 0)
     lax.fori_loop(0, leaf_dev, middle, 0)
-    side(right_ref, REACH + leaf_dev)
+    side(right_p, right_v, REACH + leaf_dev)
 
     def one(t, _):
         acc = None
@@ -138,14 +250,14 @@
     lax.fori_loop(0, leaf_dev, one, 0)
 
 
-def near_product(offsets, inverse, left, points, vectors, right):
+def near_product(offsets, inverse, left_p, left_v, points, vectors, right_p, right_v):
     dims, count = points.shape
     probes = vectors.shape[0]
-    width = count + left.shape[1] + right.shape[1]
+    width = count + left_p.shape[1] + right_p.shape[1]
     depth = 4 * dims
     return pl.pallas_call(
         near_kernel,
-        in_specs=[pl.BlockSpec(memory_space=pltpu.SMEM)] + vmem(5),
+        in_specs=[pl.BlockSpec(memory_space=pltpu.SMEM)] + vmem(7),
         out_specs=pl.BlockSpec(memory_space=pltpu.VMEM),
         out_shape=jax.ShapeDtypeStruct((probes, count), jnp.float32),
         scratch_shapes=[
@@ -155,7 +267,7 @@
         ],
         cost_estimate=pl.CostEstimate(flops=40 * 10**9, bytes_accessed=4 << 20, transcendentals=33 << 20),
         compiler_params=pltpu.CompilerParams(vmem_limit_bytes=32 << 20),
-    )(offsets, inverse, left, points, vectors, right)
+    )(offsets, inverse, left_p, left_v, points, vectors, right_p, right_v)
 
 
 def far_kernel(
@@ -295,22 +407,12 @@
     upper_coupling,
 ):
     inverse = (1.0 / lengthscale)[:, None]
-    leaf = leaf_basis.shape[2]
-    count = points.shape[1]
     seg_count = lax.axis_size("seg")
     place = lax.axis_index("seg").astype(jnp.int32)[None]
-    ahead = [(i, i + 1) for i in range(seg_count - 1)]
-    back = [(i + 1, i) for i in range(seg_count - 1)]
-    reach = REACH * leaf
-    first = jnp.concatenate([points[:, :reach], vectors[:, :reach]], axis=0)
-    last = jnp.concatenate([points[:, count - reach :], vectors[:, count - reach :]], axis=0)
-    left = lax.ppermute(last, "seg", ahead)
-    right = lax.ppermute(first, "seg", back)
-    own, head, tail, top = upward(leaf_basis, vectors, local_transfer, local_skeleton)
-    far_left = lax.ppermute(tail, "seg", ahead)
-    far_right = lax.ppermute(head, "seg", back)
-    far_top = lax.all_gather(top, "seg", axis=0, tiled=False)
-    near_part = near_product(near_offsets, inverse, left, points, vectors, right)
+    own, left_p, left_v, right_p, right_v, far_left, far_right, far_top = upward(
+        seg_count, leaf_basis, points, vectors, local_transfer, local_skeleton
+    )
+    near_part = near_product(near_offsets, inverse, left_p, left_v, points, vectors, right_p, right_v)
     return far_sum(
         seg_count, place, local_coupling, upper_coupling, inverse, leaf_basis, local_transfer, upper_transfer,
         upper_skeleton, own, far_left, far_right, far_top, near_part,

time: 95.4 us -> 84.7 us (0.89)
  blocking collectives: 23.8 us -> 0 us
  Pallas kernels: 52.6 us -> 76.3 us
  starting transfers between devices: 12.1 us -> 0 us
  local copies, waits for them, and re-layouts: 4.77 us -> 7.99 us
  other arithmetic: 1.55 us -> 0.01 us
    all_gather x1 -> x0, blocking collectives: 23.8 us -> none  [body(): far_top = lax.all_gather(top, 'seg', axis=0, tiled=False)]
    pallas_call x1, Pallas kernels: 0.97 us -> 24.6 us  [upward(): pl.pallas_call(functools.partial(upward_kernel, seg_count), in_specs=vmem...]
    ppermute x4 -> x0, starting transfers between devices: 12.1 us -> none  [the longest x1 4.66 us: body(): left = lax.ppermute(last, 'seg', ahead)]
    unnamed x29 -> x33, local copies, waits for them, and re-layouts: 3.61 us -> 7.9 us
    concatenate x2 -> x0, other arithmetic: 1.54 us -> none  [the longest x1 0.77 us: body(): jnp.concatenate([points[:, count - reach:], vectors[:, count - reach:]],...]
    slice x2 -> x0, local copies, waits for them, and re-layouts: 1.08 us -> none  [body(): first = jnp.concatenate([points[:, :reach], vectors[:, :reach]], axis=0)]
  transfers between devices with their start and end apart: 4 -> 0, of which waited for: 0 -> 0; matrix products, arithmetic and copies ran while one was open for 1% -> 0% of each run, Pallas kernels for 48% -> 0%
where the time goes in v3:
time: 84.7 us; the launch traced here: 84.3 us
  Pallas kernels  76.3 us (90%)
  local copies, waits for them, and re-layouts  7.99 us (9%)
    pallas_call x1, Pallas kernels, near_product(): pl.pallas_call(near_kernel, in_specs=[pl.BlockSpec(memory_space=pltpu.SME...  44.8 us
    pallas_call x1, Pallas kernels, upward(): pl.pallas_call(functools.partial(upward_kernel, seg_count), in_specs=vmem...  24.6 us
    unnamed x33, local copies, waits for them, and re-layouts  7.9 us
    pallas_call x1, Pallas kernels, far_sum(): pl.pallas_call(functools.partial(far_kernel, seg_count), in_specs=[pl.Blo...  6.78 us

profile of v3, /device:TPU:1, one launch (start us, length us, event | category | flops | bytes accessed | tf_op | source)
XLA Modules:
  0.0 84.3 jit_solution(4948895103817767366)
XLA Ops:
  0.0 0.0 copy-start.14
  0.0 0.7 copy-done.14
  0.7 0.0 copy-start.11
  0.7 0.1 copy.16.inv_ref
  0.7 0.6 copy-done.11
  1.4 0.0 copy-start.12
  1.4 0.1 copy.12.off_ref
  1.4 0.6 copy-done.12
  2.0 0.0 copy-start.13
  2.0 0.1 copy.15.upper_ref
  2.1 0.6 copy-done.13
  2.7 0.1 copy.14.local_ref
  2.8 0.0 copy-start
  2.8 1.2 %copy-done = bf16[16,64,512]{2,1,0:T(8,128)(2,1)S(1)} copy-done((bf16[16,64,512]{2,1,0:T(8,128)(2,1)S(1)}, bf16[16,64,512]{2,1,0:T(8,128)(2,1)}, u32[]{:S(2)}) %copy-start) | copy-done | bytes 1048600
  4.0 0.0 copy-start.2
  4.0 1.0 %copy-done.2 = bf16[32,8192]{1,0:T(8,128)(2,1)S(1)} copy-done((bf16[32,8192]{1,0:T(8,128)(2,1)S(1)}, bf16[32,8192]{1,0:T(8,128)(2,1)}, u32[]{:S(2)}) %copy-start.2) | copy-done | bytes 524312
  5.1 0.0 copy-start.4
  5.1 1.0 %copy-done.4 = bf16[30,64,64]{2,1,0:T(8,128)(2,1)S(1)} copy-done((bf16[30,64,64]{2,1,0:T(8,128)(2,1)S(1)}, bf16[30,64,64]{2,1,0:T(8,128)(2,1)}, u32[]{:S(2)}) %copy-start.4) | copy-done | bytes 245784
  6.1 0.0 copy-start.7
  6.1 0.9 %copy-done.7 = bf16[16,8192]{1,0:T(8,128)(2,1)S(1)} copy-done((bf16[16,8192]{1,0:T(8,128)(2,1)S(1)}, bf16[16,8192]{1,0:T(8,128)(2,1)}, u32[]{:S(2)}) %copy-start.7) | copy-done | bytes 262168
  7.1 0.0 copy-start.9
  7.1 0.9 %copy-done.9 = bf16[31,16,64]{2,1,0:T(8,128)(2,1)S(1)} copy-done((bf16[31,16,64]{2,1,0:T(8,128)(2,1)S(1)}, bf16[31,16,64]{2,1,0:T(8,128)(2,1)}, u32[]{:S(2)}) %copy-start.9) | copy-done | bytes 63512
  8.0 0.0 copy-start.3
  8.0 0.0 copy-start.8
  8.0 24.6 %shard_map.109 = (bf16[31,48,64]{2,1,0:T(8,128)(2,1)S(1)}, bf16[16,4096]{1,0:T(8,128)(2,1)S(1)}, bf16[32,4096]{1,0:T(8,128)(2,1)S(1)}, bf16[16,4096]{1,0:T(8,128...) custom-call(bf16[16,64,512]{2,1,0:T(8,128)(2,1)S(1)} %copy-done, ...), custom_call_target="tpu_custom_call" | custom-call | flops 4000000000 | bytes 4194304 | tf_op jit(solution)/shard_map/pallas_call | solution.py:190
  32.6 0.0 copy-done.3
  32.6 0.0 copy-done.8
  32.6 0.0 copy-start.1
  32.6 0.0 copy-start.5
  32.7 0.0 copy-start.6
  32.7 0.0 copy-start.10
  32.7 44.8 %shard_map.110.near_ref = f32[32,8192]{1,0:T(8,128)S(1)} custom-call(s32[16,8]{1,0:T(8,128)S(1)} %copy.12.off_ref, f32[16,1]{1,0:T(8,128)S(1)} %copy.16.inv_ref, bf16[16,4096]{1,0:T(8,128)(2,1)S(1)} %get-tuple-element.17.left_p, bf16[32,4096]{1,0:T(8,128)(2,1)S(1)} %get-tuple-element.18.left_v, bf16[16,8192]{1,0:T(8,128)(2,1)S(1)} %copy-done.8, ...), custom_call_target="tpu_custom_call" | custom-call | flops 40000000000 | bytes 4194304 | tf_op jit(solution)/shard_map/pallas_call | solution.py:258
  77.5 0.0 copy-done.1
  77.5 0.0 copy-done.5
  77.5 0.0 copy-done.6
  77.5 0.0 copy-done.10
  77.6 6.8 %shard_map.111 = f32[32,8192]{1,0:T(8,128)} custom-call(s32[1]{0:T(128)} %bitcast.place_ref, s32[31,4]{1,0:T(8,128)S(1)} %copy.14.local_ref, s32[12,4]{1,0:T(8,128)S(1)} %copy.15.upper_ref, f32[16,1]{1,0:T(8,128)S(1)} %copy.16.inv_ref, bf16[16,64,512]{2,1,0:T(8,128)(2,1)S(1)} %copy-done.1, bf16[30,64,64]{2,1,0:T(8,128)(2,1)S(1)} %copy-done.5, ...), custom_call_target="tpu_custom_call" | custom-call | flops 10000000000 | bytes 6291456 | tf_op jit(solution)/shard_map/pallas_call | solution.py:377
  (1 shorter events, 0.0 us)
Async XLA Ops:
  0.0 0.7 copy-start.14
  0.7 0.7 copy-start.11
  1.4 0.7 copy-start.12
  2.0 0.7 copy-start.13
  2.8 1.2 %copy-start = (bf16[16,64,512]{2,1,0:T(8,128)(2,1)S(1)}, bf16[16,64,512]{2,1,0:T(8,128)(2,1)}, u32[]{:S(2)}) copy-start(bf16[16,64,512]{2,1,0:T(8,128)(2,1)} %basis_ref.3) | copy-start | bytes 3145732
  4.0 1.0 %copy-start.2 = (bf16[32,8192]{1,0:T(8,128)(2,1)S(1)}, bf16[32,8192]{1,0:T(8,128)(2,1)}, u32[]{:S(2)}) copy-start(bf16[32,8192]{1,0:T(8,128)(2,1)} %vectors_ref.3) | copy-start | bytes 1572868
  5.1 1.0 %copy-start.4 = (bf16[30,64,64]{2,1,0:T(8,128)(2,1)S(1)}, bf16[30,64,64]{2,1,0:T(8,128)(2,1)}, u32[]{:S(2)}) copy-start(bf16[30,64,64]{2,1,0:T(8,128)(2,1)} %transfer_ref.3) | copy-start | bytes 737284
  6.1 0.9 %copy-start.7 = (bf16[16,8192]{1,0:T(8,128)(2,1)S(1)}, bf16[16,8192]{1,0:T(8,128)(2,1)}, u32[]{:S(2)}) copy-start(bf16[16,8192]{1,0:T(8,128)(2,1)} %points_ref.3) | copy-start | bytes 786436
  7.1 0.9 %copy-start.9 = (bf16[31,16,64]{2,1,0:T(8,128)(2,1)S(1)}, bf16[31,16,64]{2,1,0:T(8,128)(2,1)}, u32[]{:S(2)}) copy-start(bf16[31,16,64]{2,1,0:T(8,128)(2,1)} %skeleton_ref.1) | copy-start | bytes 190468
  8.0 24.6 %copy-start.3 = (bf16[32,8192]{1,0:T(8,128)(2,1)S(1)}, bf16[32,8192]{1,0:T(8,128)(2,1)}, u32[]{:S(2)}) copy-start(bf16[32,8192]{1,0:T(8,128)(2,1)} %vectors_ref.3) | copy-start | bytes 1572868
  8.0 24.7 %copy-start.8 = (bf16[16,8192]{1,0:T(8,128)(2,1)S(1)}, bf16[16,8192]{1,0:T(8,128)(2,1)}, u32[]{:S(2)}) copy-start(bf16[16,8192]{1,0:T(8,128)(2,1)} %points_ref.3) | copy-start | bytes 786436
  32.6 44.9 %copy-start.1 = (bf16[16,64,512]{2,1,0:T(8,128)(2,1)S(1)}, bf16[16,64,512]{2,1,0:T(8,128)(2,1)}, u32[]{:S(2)}) copy-start(bf16[16,64,512]{2,1,0:T(8,128)(2,1)} %basis_ref.3) | copy-start | bytes 3145732
  32.6 44.9 %copy-start.5 = (bf16[30,64,64]{2,1,0:T(8,128)(2,1)S(1)}, bf16[30,64,64]{2,1,0:T(8,128)(2,1)}, u32[]{:S(2)}) copy-start(bf16[30,64,64]{2,1,0:T(8,128)(2,1)} %transfer_ref.3) | copy-start | bytes 737284
  32.7 44.9 %copy-start.6 = (bf16[24,64,64]{2,1,0:T(8,128)(2,1)S(1)}, bf16[24,64,64]{2,1,0:T(8,128)(2,1)}, u32[]{:S(2)}) copy-start(bf16[24,64,64]{2,1,0:T(8,128)(2,1)} %up_transfer_ref.1) | copy-start | bytes 589828
  32.7 44.9 %copy-start.10 = (bf16[12,16,64]{2,1,0:T(8,128)(2,1)S(1)}, bf16[12,16,64]{2,1,0:T(8,128)(2,1)}, u32[]{:S(2)}) copy-start(bf16[12,16,64]{2,1,0:T(8,128)(2,1)} %up_skeleton_ref.1) | copy-start | bytes 73732

commit v4 on v3

--- a/solution.py
+++ b/solution.py
@@ -49,8 +49,8 @@
 
 def upward_kernel(
     seg_count, basis_ref, points_ref, vectors_ref, transfer_ref, skeleton_ref,
-    own, left_p, left_v, right_p, right_v, far_left, far_right, far_top,
-    head, tail, top, send, recv, top_send, top_recv,
+    own, left_p, left_v, right_p, right_v, far_left, far_right, far_top, far_root,
+    head, tail, top, root, send, recv, top_send, top_recv, root_send, root_recv,
 ):
     me = lax.axis_index("seg")
     reach = left_p.shape[1]
@@ -84,9 +84,20 @@
 
     def spread(d):
         return pltpu.make_async_remote_copy(
-            src_ref=top, dst_ref=far_top.at[me], send_sem=top_send.at[d], recv_sem=top_recv.at[d],
+            src_ref=root, dst_ref=far_root.at[me], send_sem=root_send.at[d], recv_sem=root_recv.at[d],
             device_id={"seg": lax.rem(me + d, seg_count)}, device_id_type=MESH,
         )
+
+    def nearby(k, by):
+        return pltpu.make_async_remote_copy(
+            src_ref=top, dst_ref=far_top.at[me], send_sem=top_send.at[k], recv_sem=top_recv.at[k],
+            device_id={"seg": me + by}, device_id_type=MESH,
+        )
+
+    steps = list(enumerate([by for by in range(-CPL_REACH, CPL_REACH + 1) if by != 0]))
+
+    def inside(by):
+        return me + by < seg_count if by > 0 else me + by >= 0
 
     @pl.when(me < seg_count - 1)
     def _():
@@ -126,6 +137,14 @@
             top[...] = own[row:]
             break
     far_top[me] = top[...]
+    root[...] = coefs[0]
+    far_root[me] = coefs[0]
+    for k, by in steps:
+
+        @pl.when(inside(by))
+        def _():
+            nearby(k, by).start()
+
 
     def start(d, _):
         spread(d).start()
@@ -170,6 +189,15 @@
         return 0
 
     lax.fori_loop(1, seg_count, finish, 0)
+    for k, by in steps:
+
+        @pl.when(inside(by))
+        def _():
+            nearby(k, by).wait_send()
+
+        @pl.when(inside(-by))
+        def _():
+            nearby(k, by).wait_recv()
 
 
 def vmem(count):
@@ -185,19 +213,22 @@
     high = sum(leaf_dev >> h for h in range(leaf_dev.bit_length()) if leaf_dev >> h < CPL_REACH)
     shapes = [
         (skeleton.shape[0], rows, rank), (dims, reach), (probes, reach), (dims, reach), (probes, reach),
-        (edge, rows, rank), (edge, rows, rank), (seg_count, high, rows, rank),
+        (edge, rows, rank), (edge, rows, rank), (seg_count, high, rows, rank), (seg_count, probes, rank),
     ]
     return pl.pallas_call(
         functools.partial(upward_kernel, seg_count),
         in_specs=vmem(5),
-        out_specs=vmem(8),
+        out_specs=vmem(9),
         out_shape=[jax.ShapeDtypeStruct(s, jnp.bfloat16) for s in shapes],
         scratch_shapes=[
             pltpu.VMEM((edge, rows, rank), jnp.bfloat16),
             pltpu.VMEM((edge, rows, rank), jnp.bfloat16),
             pltpu.VMEM((high, rows, rank), jnp.bfloat16),
+            pltpu.VMEM((probes, rank), jnp.bfloat16),
             pltpu.SemaphoreType.DMA((6,)),
             pltpu.SemaphoreType.DMA((6,)),
+            pltpu.SemaphoreType.DMA((2 * CPL_REACH,)),
+            pltpu.SemaphoreType.DMA((2 * CPL_REACH,)),
             pltpu.SemaphoreType.DMA((seg_count,)),
             pltpu.SemaphoreType.DMA((seg_count,)),
         ],
@@ -272,7 +303,7 @@
 
 def far_kernel(
     seg_count, place_ref, local_ref, upper_ref, inv_ref, basis_ref, transfer_ref, up_transfer_ref, up_skeleton_ref,
-    own_ref, left_ref, right_ref, top_ref, near_ref, out_ref, win, high, src, tgt,
+    own_ref, left_ref, right_ref, top_ref, root_ref, near_ref, out_ref, win, high, src, tgt,
 ):
     leaf_dev, rank, leaf = basis_ref.shape
     probes = near_ref.shape[0]
@@ -311,9 +342,8 @@
         below = store + pad
         store += 2 * pad + 2 * boxes
         for b in range(boxes):
-            c = mul(high[below + 2 * b, 0:probes, :], up_transfer_ref[row + 2 * b]) + mul(
-                high[below + 2 * b + 1, 0:probes, :], up_transfer_ref[row + 2 * b + 1]
-            )
+            pair = [root_ref[i] if above == 1 else high[below + i, 0:probes, :] for i in (2 * b, 2 * b + 1)]
+            c = mul(pair[0], up_transfer_ref[row + 2 * b]) + mul(pair[1], up_transfer_ref[row + 2 * b + 1])
             high[store + pad + b, 0:probes, :] = c.astype(jnp.bfloat16)
             high[store + pad + b, probes:, :] = up_skeleton_ref[skel_row + b]
         starts.append(at)
@@ -364,7 +394,7 @@
 
 def far_sum(
     seg_count, place, local_coupling, upper_coupling, inverse, leaf_basis, local_transfer, upper_transfer,
-    upper_skeleton, own, left, right, top, near_part,
+    upper_skeleton, own, left, right, top, root, near_part,
 ):
     leaf_dev, rank, _ = leaf_basis.shape
     rows = own.shape[1]
@@ -376,7 +406,7 @@
     high = sum(n * seg_count + pad for n in counts if n < CPL_REACH) + sum(n + pad for n in uppers)
     return pl.pallas_call(
         functools.partial(far_kernel, seg_count),
-        in_specs=[pl.BlockSpec(memory_space=pltpu.SMEM)] * 3 + vmem(10),
+        in_specs=[pl.BlockSpec(memory_space=pltpu.SMEM)] * 3 + vmem(11),
         out_specs=pl.BlockSpec(memory_space=pltpu.VMEM),
         out_shape=jax.ShapeDtypeStruct(near_part.shape, jnp.float32),
         scratch_shapes=[
@@ -389,7 +419,7 @@
         compiler_params=pltpu.CompilerParams(vmem_limit_bytes=40 << 20),
     )(
         place, local_coupling, upper_coupling, inverse, leaf_basis, local_transfer, upper_transfer, upper_skeleton,
-        own, left, right, top, near_part,
+        own, left, right, top, root, near_part,
     )
 
 
@@ -409,13 +439,13 @@
     inverse = (1.0 / lengthscale)[:, None]
     seg_count = lax.axis_size("seg")
     place = lax.axis_index("seg").astype(jnp.int32)[None]
-    own, left_p, left_v, right_p, right_v, far_left, far_right, far_top = upward(
+    own, left_p, left_v, right_p, right_v, far_left, far_right, far_top, far_root = upward(
         seg_count, leaf_basis, points, vectors, local_transfer, local_skeleton
     )
     near_part = near_product(near_offsets, inverse, left_p, left_v, points, vectors, right_p, right_v)
     return far_sum(
         seg_count, place, local_coupling, upper_coupling, inverse, leaf_basis, local_transfer, upper_transfer,
-        upper_skeleton, own, far_left, far_right, far_top, near_part,
+        upper_skeleton, own, far_left, far_right, far_top, far_root, near_part,
     )
 
 

time: 84.7 us -> 83.1 us (0.981)
  Pallas kernels: 76.3 us -> 74.6 us
    pallas_call x1, Pallas kernels: 24.6 us -> 23 us  [upward(): pl.pallas_call(functools.partial(upward_kernel, seg_count), in_specs=vmem...]
where the time goes in v4:
time: 83.1 us; the launch traced here: 82.7 us
  Pallas kernels  74.6 us (90%)
  local copies, waits for them, and re-layouts  7.99 us (10%)
    pallas_call x1, Pallas kernels, near_product(): pl.pallas_call(near_kernel, in_specs=[pl.BlockSpec(memory_space=pltpu.SME...  44.9 us
    pallas_call x1, Pallas kernels, upward(): pl.pallas_call(functools.partial(upward_kernel, seg_count), in_specs=vmem...  23 us
    unnamed x33, local copies, waits for them, and re-layouts  7.9 us
    pallas_call x1, Pallas kernels, far_sum(): pl.pallas_call(functools.partial(far_kernel, seg_count), in_specs=[pl.Blo...  6.74 us

profile of v4, /device:TPU:1, one launch (start us, length us, event | category | flops | bytes accessed | tf_op | source)
XLA Modules:
  0.0 82.7 jit_solution(14503797823973285104)
XLA Ops:
  0.0 0.0 copy-start.14
  0.0 0.7 copy-done.14
  0.7 0.0 copy-start.11
  0.7 0.1 copy.16.inv_ref
  0.7 0.6 copy-done.11
  1.4 0.0 copy-start.12
  1.4 0.1 copy.12.off_ref
  1.4 0.6 copy-done.12
  2.0 0.0 copy-start.13
  2.0 0.1 copy.15.upper_ref
  2.1 0.6 copy-done.13
  2.7 0.1 copy.14.local_ref
  2.8 0.0 copy-start
  2.8 1.2 %copy-done = bf16[16,64,512]{2,1,0:T(8,128)(2,1)S(1)} copy-done((bf16[16,64,512]{2,1,0:T(8,128)(2,1)S(1)}, bf16[16,64,512]{2,1,0:T(8,128)(2,1)}, u32[]{:S(2)}) %copy-start) | copy-done | bytes 1048600
  4.0 0.0 copy-start.2
  4.0 1.0 %copy-done.2 = bf16[32,8192]{1,0:T(8,128)(2,1)S(1)} copy-done((bf16[32,8192]{1,0:T(8,128)(2,1)S(1)}, bf16[32,8192]{1,0:T(8,128)(2,1)}, u32[]{:S(2)}) %copy-start.2) | copy-done | bytes 524312
  5.1 0.0 copy-start.4
  5.1 1.0 %copy-done.4 = bf16[30,64,64]{2,1,0:T(8,128)(2,1)S(1)} copy-done((bf16[30,64,64]{2,1,0:T(8,128)(2,1)S(1)}, bf16[30,64,64]{2,1,0:T(8,128)(2,1)}, u32[]{:S(2)}) %copy-start.4) | copy-done | bytes 245784
  6.1 0.0 copy-start.7
  6.1 0.9 %copy-done.7 = bf16[16,8192]{1,0:T(8,128)(2,1)S(1)} copy-done((bf16[16,8192]{1,0:T(8,128)(2,1)S(1)}, bf16[16,8192]{1,0:T(8,128)(2,1)}, u32[]{:S(2)}) %copy-start.7) | copy-done | bytes 262168
  7.1 0.0 copy-start.9
  7.1 0.9 %copy-done.9 = bf16[31,16,64]{2,1,0:T(8,128)(2,1)S(1)} copy-done((bf16[31,16,64]{2,1,0:T(8,128)(2,1)S(1)}, bf16[31,16,64]{2,1,0:T(8,128)(2,1)}, u32[]{:S(2)}) %copy-start.9) | copy-done | bytes 63512
  8.0 0.0 copy-start.3
  8.0 0.0 copy-start.8
  8.0 23.0 %shard_map.109 = (bf16[31,48,64]{2,1,0:T(8,128)(2,1)S(1)}, bf16[16,4096]{1,0:T(8,128)(2,1)S(1)}, bf16[32,4096]{1,0:T(8,128)(2,1)S(1)}, bf16[16,4096]{1,0:T(8,128...) custom-call(bf16[16,64,512]{2,1,0:T(8,128)(2,1)S(1)} %copy-done, ...), custom_call_target="tpu_custom_call" | custom-call | flops 4000000000 | bytes 4194304 | tf_op jit(solution)/shard_map/pallas_call | solution.py:218
  31.0 0.0 copy-done.3
  31.0 0.0 copy-done.8
  31.0 0.0 copy-start.1
  31.0 0.0 copy-start.5
  31.1 0.0 copy-start.6
  31.1 0.0 copy-start.10
  31.1 44.9 %shard_map.110.near_ref = f32[32,8192]{1,0:T(8,128)S(1)} custom-call(s32[16,8]{1,0:T(8,128)S(1)} %copy.12.off_ref, f32[16,1]{1,0:T(8,128)S(1)} %copy.16.inv_ref, bf16[16,4096]{1,0:T(8,128)(2,1)S(1)} %get-tuple-element.19.left_p, bf16[32,4096]{1,0:T(8,128)(2,1)S(1)} %get-tuple-element.20.left_v, bf16[16,8192]{1,0:T(8,128)(2,1)S(1)} %copy-done.8, ...), custom_call_target="tpu_custom_call" | custom-call | flops 40000000000 | bytes 4194304 | tf_op jit(solution)/shard_map/pallas_call | solution.py:289
  75.9 0.0 copy-done.1
  75.9 0.0 copy-done.5
  76.0 0.0 copy-done.6
  76.0 0.0 copy-done.10
  76.0 6.7 %shard_map.111 = f32[32,8192]{1,0:T(8,128)} custom-call(s32[1]{0:T(128)} %bitcast.place_ref, s32[31,4]{1,0:T(8,128)S(1)} %copy.14.local_ref, s32[12,4]{1,0:T(8,128)S(1)} %copy.15.upper_ref, f32[16,1]{1,0:T(8,128)S(1)} %copy.16.inv_ref, bf16[16,64,512]{2,1,0:T(8,128)(2,1)S(1)} %copy-done.1, bf16[30,64,64]{2,1,0:T(8,128)(2,1)S(1)} %copy-done.5, ...), custom_call_target="tpu_custom_call" | custom-call | flops 10000000000 | bytes 6291456 | tf_op jit(solution)/shard_map/pallas_call | solution.py:407
  (1 shorter events, 0.0 us)
Async XLA Ops:
  0.0 0.7 copy-start.14
  0.7 0.7 copy-start.11
  1.4 0.7 copy-start.12
  2.0 0.7 copy-start.13
  2.8 1.2 %copy-start = (bf16[16,64,512]{2,1,0:T(8,128)(2,1)S(1)}, bf16[16,64,512]{2,1,0:T(8,128)(2,1)}, u32[]{:S(2)}) copy-start(bf16[16,64,512]{2,1,0:T(8,128)(2,1)} %basis_ref.3) | copy-start | bytes 3145732
  4.0 1.0 %copy-start.2 = (bf16[32,8192]{1,0:T(8,128)(2,1)S(1)}, bf16[32,8192]{1,0:T(8,128)(2,1)}, u32[]{:S(2)}) copy-start(bf16[32,8192]{1,0:T(8,128)(2,1)} %vectors_ref.3) | copy-start | bytes 1572868
  5.1 1.0 %copy-start.4 = (bf16[30,64,64]{2,1,0:T(8,128)(2,1)S(1)}, bf16[30,64,64]{2,1,0:T(8,128)(2,1)}, u32[]{:S(2)}) copy-start(bf16[30,64,64]{2,1,0:T(8,128)(2,1)} %transfer_ref.3) | copy-start | bytes 737284
  6.1 0.9 %copy-start.7 = (bf16[16,8192]{1,0:T(8,128)(2,1)S(1)}, bf16[16,8192]{1,0:T(8,128)(2,1)}, u32[]{:S(2)}) copy-start(bf16[16,8192]{1,0:T(8,128)(2,1)} %points_ref.3) | copy-start | bytes 786436
  7.1 0.9 %copy-start.9 = (bf16[31,16,64]{2,1,0:T(8,128)(2,1)S(1)}, bf16[31,16,64]{2,1,0:T(8,128)(2,1)}, u32[]{:S(2)}) copy-start(bf16[31,16,64]{2,1,0:T(8,128)(2,1)} %skeleton_ref.1) | copy-start | bytes 190468
  8.0 23.1 %copy-start.3 = (bf16[32,8192]{1,0:T(8,128)(2,1)S(1)}, bf16[32,8192]{1,0:T(8,128)(2,1)}, u32[]{:S(2)}) copy-start(bf16[32,8192]{1,0:T(8,128)(2,1)} %vectors_ref.3) | copy-start | bytes 1572868
  8.0 23.1 %copy-start.8 = (bf16[16,8192]{1,0:T(8,128)(2,1)S(1)}, bf16[16,8192]{1,0:T(8,128)(2,1)}, u32[]{:S(2)}) copy-start(bf16[16,8192]{1,0:T(8,128)(2,1)} %points_ref.3) | copy-start | bytes 786436
  31.0 44.9 %copy-start.1 = (bf16[16,64,512]{2,1,0:T(8,128)(2,1)S(1)}, bf16[16,64,512]{2,1,0:T(8,128)(2,1)}, u32[]{:S(2)}) copy-start(bf16[16,64,512]{2,1,0:T(8,128)(2,1)} %basis_ref.3) | copy-start | bytes 3145732
  31.0 44.9 %copy-start.5 = (bf16[30,64,64]{2,1,0:T(8,128)(2,1)S(1)}, bf16[30,64,64]{2,1,0:T(8,128)(2,1)}, u32[]{:S(2)}) copy-start(bf16[30,64,64]{2,1,0:T(8,128)(2,1)} %transfer_ref.3) | copy-start | bytes 737284
  31.1 44.9 %copy-start.6 = (bf16[24,64,64]{2,1,0:T(8,128)(2,1)S(1)}, bf16[24,64,64]{2,1,0:T(8,128)(2,1)}, u32[]{:S(2)}) copy-start(bf16[24,64,64]{2,1,0:T(8,128)(2,1)} %up_transfer_ref.1) | copy-start | bytes 589828
  31.1 44.9 %copy-start.10 = (bf16[12,16,64]{2,1,0:T(8,128)(2,1)S(1)}, bf16[12,16,64]{2,1,0:T(8,128)(2,1)}, u32[]{:S(2)}) copy-start(bf16[12,16,64]{2,1,0:T(8,128)(2,1)} %up_skeleton_ref.1) | copy-start | bytes 73732

commit v5 on v4

--- a/solution.py
+++ b/solution.py
@@ -270,10 +270,11 @@
     def one(t, _):
         acc = None
         target = tgt[:, part(t)]
-        for m in range(near):
-            col = part(t + REACH + off_ref[t, m])
-            k = jnp.exp2(mul(src[col, :], target)).astype(jnp.bfloat16)
-            d = mul(vec[:, col], k)
+        for m in range(0, near, 2):
+            cols = [part(t + REACH + off_ref[t, n]) for n in range(m, min(m + 2, near))]
+            source = jnp.concatenate([src[col, :] for col in cols], axis=0)
+            k = jnp.exp2(mul(source, target)).astype(jnp.bfloat16)
+            d = mul(jnp.concatenate([vec[:, col] for col in cols], axis=1), k)
             acc = d if acc is None else acc + d
         out_ref[:, part(t)] = acc
         return 0

time: 83.1 us -> 75.2 us (0.905)
  Pallas kernels: 74.6 us -> 66.8 us
    pallas_call x1, Pallas kernels: 44.9 us -> 37 us  [near_product(): pl.pallas_call(near_kernel, in_specs=[pl.BlockSpec(memory_space=pltpu.SME...]
where the time goes in v5:
time: 75.2 us; the launch traced here: 74.8 us
  Pallas kernels  66.8 us (89%)
  local copies, waits for them, and re-layouts  7.99 us (11%)
    pallas_call x1, Pallas kernels, near_product(): pl.pallas_call(near_kernel, in_specs=[pl.BlockSpec(memory_space=pltpu.SME...  37 us
    pallas_call x1, Pallas kernels, upward(): pl.pallas_call(functools.partial(upward_kernel, seg_count), in_specs=vmem...  23 us
    unnamed x33, local copies, waits for them, and re-layouts  7.9 us
    pallas_call x1, Pallas kernels, far_sum(): pl.pallas_call(functools.partial(far_kernel, seg_count), in_specs=[pl.Blo...  6.74 us

profile of v5, /device:TPU:1, one launch (start us, length us, event | category | flops | bytes accessed | tf_op | source)
XLA Modules:
  0.0 74.8 jit_solution(13921114520526485356)
XLA Ops:
  0.0 0.0 copy-start.14
  0.0 0.7 copy-done.14
  0.7 0.0 copy-start.11
  0.7 0.1 copy.16.inv_ref
  0.7 0.6 copy-done.11
  1.4 0.0 copy-start.12
  1.4 0.1 copy.12.off_ref
  1.4 0.6 copy-done.12
  2.0 0.0 copy-start.13
  2.0 0.1 copy.15.upper_ref
  2.1 0.6 copy-done.13
  2.7 0.1 copy.14.local_ref
  2.8 0.0 copy-start
  2.8 1.2 %copy-done = bf16[16,64,512]{2,1,0:T(8,128)(2,1)S(1)} copy-done((bf16[16,64,512]{2,1,0:T(8,128)(2,1)S(1)}, bf16[16,64,512]{2,1,0:T(8,128)(2,1)}, u32[]{:S(2)}) %copy-start) | copy-done | bytes 1048600
  4.0 0.0 copy-start.2
  4.0 1.0 %copy-done.2 = bf16[32,8192]{1,0:T(8,128)(2,1)S(1)} copy-done((bf16[32,8192]{1,0:T(8,128)(2,1)S(1)}, bf16[32,8192]{1,0:T(8,128)(2,1)}, u32[]{:S(2)}) %copy-start.2) | copy-done | bytes 524312
  5.1 0.0 copy-start.4
  5.1 1.0 %copy-done.4 = bf16[30,64,64]{2,1,0:T(8,128)(2,1)S(1)} copy-done((bf16[30,64,64]{2,1,0:T(8,128)(2,1)S(1)}, bf16[30,64,64]{2,1,0:T(8,128)(2,1)}, u32[]{:S(2)}) %copy-start.4) | copy-done | bytes 245784
  6.1 0.0 copy-start.7
  6.1 0.9 %copy-done.7 = bf16[16,8192]{1,0:T(8,128)(2,1)S(1)} copy-done((bf16[16,8192]{1,0:T(8,128)(2,1)S(1)}, bf16[16,8192]{1,0:T(8,128)(2,1)}, u32[]{:S(2)}) %copy-start.7) | copy-done | bytes 262168
  7.1 0.0 copy-start.9
  7.1 0.9 %copy-done.9 = bf16[31,16,64]{2,1,0:T(8,128)(2,1)S(1)} copy-done((bf16[31,16,64]{2,1,0:T(8,128)(2,1)S(1)}, bf16[31,16,64]{2,1,0:T(8,128)(2,1)}, u32[]{:S(2)}) %copy-start.9) | copy-done | bytes 63512
  8.0 0.0 copy-start.3
  8.0 0.0 copy-start.8
  8.0 23.0 %shard_map.109 = (bf16[31,48,64]{2,1,0:T(8,128)(2,1)S(1)}, bf16[16,4096]{1,0:T(8,128)(2,1)S(1)}, bf16[32,4096]{1,0:T(8,128)(2,1)S(1)}, bf16[16,4096]{1,0:T(8,128...) custom-call(bf16[16,64,512]{2,1,0:T(8,128)(2,1)S(1)} %copy-done, ...), custom_call_target="tpu_custom_call" | custom-call | flops 4000000000 | bytes 4194304 | tf_op jit(solution)/shard_map/pallas_call | solution.py:218
  31.0 0.0 copy-done.3
  31.0 0.0 copy-done.8
  31.0 0.0 copy-start.1
  31.0 0.0 copy-start.5
  31.1 0.0 copy-start.6
  31.1 0.0 copy-start.10
  31.1 37.0 %shard_map.110.near_ref = f32[32,8192]{1,0:T(8,128)S(1)} custom-call(s32[16,8]{1,0:T(8,128)S(1)} %copy.12.off_ref, f32[16,1]{1,0:T(8,128)S(1)} %copy.16.inv_ref, bf16[16,4096]{1,0:T(8,128)(2,1)S(1)} %get-tuple-element.19.left_p, bf16[32,4096]{1,0:T(8,128)(2,1)S(1)} %get-tuple-element.20.left_v, bf16[16,8192]{1,0:T(8,128)(2,1)S(1)} %copy-done.8, ...), custom_call_target="tpu_custom_call" | custom-call | flops 40000000000 | bytes 4194304 | tf_op jit(solution)/shard_map/pallas_call | solution.py:290
  68.1 0.0 copy-done.1
  68.1 0.0 copy-done.5
  68.1 0.0 copy-done.6
  68.1 0.0 copy-done.10
  68.1 6.7 %shard_map.111 = f32[32,8192]{1,0:T(8,128)} custom-call(s32[1]{0:T(128)} %bitcast.place_ref, s32[31,4]{1,0:T(8,128)S(1)} %copy.14.local_ref, s32[12,4]{1,0:T(8,128)S(1)} %copy.15.upper_ref, f32[16,1]{1,0:T(8,128)S(1)} %copy.16.inv_ref, bf16[16,64,512]{2,1,0:T(8,128)(2,1)S(1)} %copy-done.1, bf16[30,64,64]{2,1,0:T(8,128)(2,1)S(1)} %copy-done.5, ...), custom_call_target="tpu_custom_call" | custom-call | flops 10000000000 | bytes 6291456 | tf_op jit(solution)/shard_map/pallas_call | solution.py:408
  (1 shorter events, 0.0 us)
Async XLA Ops:
  0.0 0.7 copy-start.14
  0.7 0.7 copy-start.11
  1.4 0.7 copy-start.12
  2.0 0.7 copy-start.13
  2.8 1.2 %copy-start = (bf16[16,64,512]{2,1,0:T(8,128)(2,1)S(1)}, bf16[16,64,512]{2,1,0:T(8,128)(2,1)}, u32[]{:S(2)}) copy-start(bf16[16,64,512]{2,1,0:T(8,128)(2,1)} %basis_ref.3) | copy-start | bytes 3145732
  4.0 1.0 %copy-start.2 = (bf16[32,8192]{1,0:T(8,128)(2,1)S(1)}, bf16[32,8192]{1,0:T(8,128)(2,1)}, u32[]{:S(2)}) copy-start(bf16[32,8192]{1,0:T(8,128)(2,1)} %vectors_ref.3) | copy-start | bytes 1572868
  5.1 1.0 %copy-start.4 = (bf16[30,64,64]{2,1,0:T(8,128)(2,1)S(1)}, bf16[30,64,64]{2,1,0:T(8,128)(2,1)}, u32[]{:S(2)}) copy-start(bf16[30,64,64]{2,1,0:T(8,128)(2,1)} %transfer_ref.3) | copy-start | bytes 737284
  6.1 0.9 %copy-start.7 = (bf16[16,8192]{1,0:T(8,128)(2,1)S(1)}, bf16[16,8192]{1,0:T(8,128)(2,1)}, u32[]{:S(2)}) copy-start(bf16[16,8192]{1,0:T(8,128)(2,1)} %points_ref.3) | copy-start | bytes 786436
  7.1 0.9 %copy-start.9 = (bf16[31,16,64]{2,1,0:T(8,128)(2,1)S(1)}, bf16[31,16,64]{2,1,0:T(8,128)(2,1)}, u32[]{:S(2)}) copy-start(bf16[31,16,64]{2,1,0:T(8,128)(2,1)} %skeleton_ref.1) | copy-start | bytes 190468
  8.0 23.1 %copy-start.3 = (bf16[32,8192]{1,0:T(8,128)(2,1)S(1)}, bf16[32,8192]{1,0:T(8,128)(2,1)}, u32[]{:S(2)}) copy-start(bf16[32,8192]{1,0:T(8,128)(2,1)} %vectors_ref.3) | copy-start | bytes 1572868
  8.0 23.1 %copy-start.8 = (bf16[16,8192]{1,0:T(8,128)(2,1)S(1)}, bf16[16,8192]{1,0:T(8,128)(2,1)}, u32[]{:S(2)}) copy-start(bf16[16,8192]{1,0:T(8,128)(2,1)} %points_ref.3) | copy-start | bytes 786436
  31.0 37.0 %copy-start.1 = (bf16[16,64,512]{2,1,0:T(8,128)(2,1)S(1)}, bf16[16,64,512]{2,1,0:T(8,128)(2,1)}, u32[]{:S(2)}) copy-start(bf16[16,64,512]{2,1,0:T(8,128)(2,1)} %basis_ref.3) | copy-start | bytes 3145732
  31.0 37.0 %copy-start.5 = (bf16[30,64,64]{2,1,0:T(8,128)(2,1)S(1)}, bf16[30,64,64]{2,1,0:T(8,128)(2,1)}, u32[]{:S(2)}) copy-start(bf16[30,64,64]{2,1,0:T(8,128)(2,1)} %transfer_ref.3) | copy-start | bytes 737284
  31.1 37.0 %copy-start.6 = (bf16[24,64,64]{2,1,0:T(8,128)(2,1)S(1)}, bf16[24,64,64]{2,1,0:T(8,128)(2,1)}, u32[]{:S(2)}) copy-start(bf16[24,64,64]{2,1,0:T(8,128)(2,1)} %up_transfer_ref.1) | copy-start | bytes 589828
  31.1 37.0 %copy-start.10 = (bf16[12,16,64]{2,1,0:T(8,128)(2,1)S(1)}, bf16[12,16,64]{2,1,0:T(8,128)(2,1)}, u32[]{:S(2)}) copy-start(bf16[12,16,64]{2,1,0:T(8,128)(2,1)} %up_skeleton_ref.1) | copy-start | bytes 73732
